TPU v7x, 32 devices: a whole 2x2x4 slice. The times are simulated.
32 devices in a mesh: leaf: 8 (over z, y), panel: 4 (over x, core).
Axes of the slice: x: 2, y: 2, z: 4, core: 2. Of those that a mesh axis runs over, the one named last changes fastest.
Arguments:
- border: bfloat16 [8, 128, 8192], P('leaf', 'panel'), may hold values from -0.1875 to 0.1875
- solution: bfloat16 [8, 128, 128], P('leaf', 'panel'), may hold values from -6 to 6
- winv_top: bfloat16 [4096, 4096], P(None, ('leaf', 'panel')), as said below
- winv_mid: bfloat16 [4096, 8192], P(None, ('leaf', 'panel')), as said below
- coupling: bfloat16 [8192, 4096], P(('leaf', 'panel')), may hold values from -0.0625 to 0.0625
Outputs:
- top_adjoint: float32 [4096, 128], P(('leaf', 'panel'))
- mid_adjoint: float32 [8192, 128], P(('leaf', 'panel'))
Inputs may be any that keep to these rules, and one draw needn't show every extreme that they name: `winv_top`: each 4096 x 4096 block of the factor is lower triangular with a positive diagonal. `winv_mid`: each 4096 x 4096 block of the factor is lower triangular with a positive diagonal.
All inputs are finite; a program needn't handle non-finite values.
Results may differ from a plain program's by a relative error of at most 0.0003.
Values sent between devices are 32-bit elements; how exact they have to be, the bound alone decides.
No kernel may reach another device: no remote copies, remote signals or barrier semaphores. Data moves between devices by JAX's collectives and lax.ppermute only.
A program may use at most 64 MiB of HBM per device.

v0:
```python
import functools

import jax
import jax.numpy as jnp
from jax import lax
from jax.experimental import pallas as pl
from jax.experimental.pallas import tpu as pltpu
from jax.sharding import PartitionSpec as P

AXES = ("leaf", "panel")
F32 = jnp.float32
BF16 = jnp.bfloat16
LANES = 128


def plain_body(border, solution, winv_top, winv_mid, coupling):
    leaves = lax.axis_size("leaf")
    panels = lax.axis_size("panel")
    half = leaves // 2
    leaf_id = lax.axis_index("leaf")
    front = winv_top.shape[0]
    top_cols = winv_top.shape[1]
    mid_cols = winv_mid.shape[1]
    contribution = lax.dot_general(
        border[0], solution[0], (((0,), (0,)), ((), ())), preferred_element_type=F32
    )
    groups = [list(range(half)), list(range(half, leaves))]
    device = leaf_id * panels + lax.axis_index("panel")
    in_half = device % (half * panels)
    top_load = lax.psum(contribution[:front], AXES)
    top_block = lax.dynamic_slice_in_dim(top_load, device * top_cols, top_cols, 0)
    mid_load = lax.psum(contribution[front:], "panel")
    mid_load = lax.psum(mid_load, "leaf", axis_index_groups=groups)
    mid_block = lax.dynamic_slice_in_dim(mid_load, in_half * mid_cols, mid_cols, 0)
    top_factor = winv_top.astype(F32)
    mid_factor = winv_mid.astype(F32)
    exact = lax.Precision.HIGHEST
    top_inner = lax.psum(jnp.dot(top_factor, top_block, precision=exact), AXES)
    top_adjoint = jnp.dot(top_factor.T, top_inner, precision=exact)
    top_whole = lax.all_gather(top_adjoint, AXES, axis=0, tiled=True)
    mid_rhs = mid_block - jnp.dot(coupling.astype(F32), top_whole, precision=exact)
    mid_inner = lax.psum(jnp.dot(mid_factor, mid_rhs, precision=exact), "panel")
    mid_inner = lax.psum(mid_inner, "leaf", axis_index_groups=groups)
    mid_adjoint = jnp.dot(mid_factor.T, mid_inner, precision=exact)
    return top_adjoint, mid_adjoint


WIDE = 64
CORE, XBIT, YBIT, NEAR, FAR = 1, 2, 4, 8, 16


def permute(value, partner):
    return lax.ppermute(value, AXES, [(i, partner(i)) for i in range(32)])


def swap(value, mask):
    return permute(value, lambda i: i ^ mask)


def swap_first(value, colour):
    return swap(value, YBIT if colour else XBIT)


def swap_second(value, colour):
    return swap(value, XBIT if colour else YBIT)


def coords():
    leaf = lax.axis_index("leaf")
    panel = lax.axis_index("panel")
    return leaf // 2, leaf % 2, panel // 2, panel % 2


def flip(a, k):
    return a + k - 2 * a * k


def z_flip(z, k):
    return flip(z // 2, k // 2) * 2 + flip(z % 2, k % 2)


Z_ORDER = (0, 2, 1, 3)


def plane_at(y, x, colour, first, second):
    along_x = first * (1 - colour) + second * colour
    along_y = first * colour + second * (1 - colour)
    return flip(y, along_y) * 2 + flip(x, along_x)


def block_starts(deep, colour):
    z, y, x, c = coords()
    core = flip(c, colour)
    starts = []
    for first in range(2):
        for second in range(2):
            plane = plane_at(y, x, colour, first, second)
            for j in range(4):
                if deep:
                    start = ((z_flip(z, Z_ORDER[j]) * 4 + plane) * 2 + core) * 128
                else:
                    start = ((flip(z % 2, j // 2) * 4 + plane) * 2 + core) * 256 + j % 2 * 128
                starts.append(pl.multiple_of(start, 128))
    return starts


def size_of(array):
    return array.size * array.dtype.itemsize


def kernel_call(kernel, outs, ins, scratch=(), flops=0, limit=10, after=()):
    vmem = pl.BlockSpec(memory_space=pltpu.VMEM)
    shapes = [jax.ShapeDtypeStruct(*o) for o in outs]

    def ordered(*refs):
        kernel(*refs[: len(ins)], *refs[len(ins) + len(after) :])

    return pl.pallas_call(
        ordered,
        out_shape=shapes,
        in_specs=[vmem] * len(ins) + [pl.BlockSpec(memory_space=pl.ANY)] * len(after),
        out_specs=[vmem] * len(outs),
        scratch_shapes=list(scratch),
        compiler_params=pltpu.CompilerParams(vmem_limit_bytes=limit * 2**20),
        cost_estimate=pl.CostEstimate(
            flops=flops,
            transcendentals=0,
            bytes_accessed=sum(map(size_of, [*ins, *shapes])),
        ),
    )(*ins, *after)


def glue(fn, *ins, after=()):
    shapes = jax.eval_shape(fn, *ins)

    def kernel(*refs):
        values = fn(*[r[...] for r in refs[: len(ins)]])
        for ref, value in zip(refs[len(ins) :], values):
            ref[...] = value

    return kernel_call(kernel, [(o.shape, o.dtype) for o in shapes], ins, after=after)


def left_lanes(shape):
    return lax.broadcasted_iota(jnp.int32, shape, 1) < WIDE


def pack(low, high):
    left = left_lanes(low.shape)
    return (
        jnp.where(left, low, pltpu.roll(high, WIDE, 1)),
        jnp.where(left, pltpu.roll(low, WIDE, 1), high),
    )


def put_split(rhs_ref, start, block):
    left = left_lanes(block.shape)
    turned = pltpu.roll(block, WIDE, 1)
    for i, rows in enumerate((jnp.where(left, block, turned), jnp.where(left, turned, block))):
        high = rows.astype(BF16).astype(F32)
        both = jnp.where(left, high, rows - high)
        rhs_ref[pl.ds(start + i * WIDE, WIDE), :] = both.astype(BF16)


def product(w, rhs_ref):
    both = jnp.dot(w, rhs_ref[...], preferred_element_type=F32)
    return both + pltpu.roll(both, WIDE, 1)


def take_block(total, start):
    low = total[start : start + WIDE]
    high = total[start + WIDE : start + 2 * WIDE]
    return jnp.where(left_lanes(low.shape), low, high)


def prep_top(border_ref, sol_ref, *tops):
    z, y, x, c = coords()
    sol = sol_ref[...].astype(F32)
    for rel in range(4):
        core = flip(c, rel % 2)
        for second in range(2):
            plane = plane_at(y, x, core, rel // 2, second)
            for j in range(4):
                col = pl.multiple_of((z_flip(z, Z_ORDER[j]) * 8 + plane * 2 + core) * 128, 128)
                here = (second * 4 + j) * 128
                tops[rel][:, here : here + 128] = border_ref[:, pl.ds(col, 128)].astype(F32)
        tops[rel][:, 1024:] = sol


def prep_mid(border_ref, *mids):
    z, y, x, c = coords()
    front = border_ref.shape[1] // 2
    for rel in range(4):
        core = flip(c, rel % 2)
        for second in range(2):
            plane = plane_at(y, x, core, rel // 2, second)
            for k in range(2):
                col = front + (flip(z % 2, k) * 8 + plane * 2 + core) * 256
                here = (second * 2 + k) * 256
                mids[rel][:, here : here + 256] = border_ref[
                    :, pl.ds(pl.multiple_of(col, 256), 256)
                ].astype(F32)


def plane_inputs(parts):
    return [
        parts[0],
        swap(parts[1], CORE),
        permute(parts[2], lambda i: i ^ (YBIT if i & 1 else XBIT)),
        permute(parts[3], lambda i: i ^ (XBIT + CORE if i & 1 else YBIT + CORE)),
    ]


def swap_loads(value):
    return permute(value, lambda i: i ^ (XBIT if i & 1 else YBIT))


def stack_rows(refs, cols, out_ref):
    n = refs[0].shape[0]
    for i, ref in enumerate(refs):
        out_ref[i * n : (i + 1) * n, :] = ref[:, cols].astype(BF16)


def put_loads(sol, rows, outs):
    total = lax.dot_general(
        sol, rows, (((0,), (0,)), ((), ())), preferred_element_type=F32
    )
    for second in range(2):
        for j in range(4):
            here = (second * 4 + j) * 128
            block = total[:, here : here + 128].T
            for h, packed in enumerate(pack(block[:WIDE], block[WIDE:])):
                outs[second][j, h] = packed


def top_load_kernel(*refs):
    ins, (keep_ref, send_ref, sol_ref, rows_ref) = refs[:4], refs[4:]
    stack_rows(ins, slice(0, 1024), rows_ref)
    stack_rows(ins, slice(1024, 1152), sol_ref)
    put_loads(sol_ref[...], rows_ref[...], [keep_ref, send_ref])


def mid_load_kernel(*refs):
    ins, (sol_ref, keep_ref, send_ref, rows_ref) = refs[:4], refs[4:]
    stack_rows(ins, slice(0, 1024), rows_ref)
    put_loads(sol_ref[...], rows_ref[...], [keep_ref, send_ref])


def widen_kernel(w_ref, out_ref):
    out_ref[...] = w_ref[...].astype(F32)


def widen(w, after=()):
    return kernel_call(widen_kernel, [(w.shape, F32)], [w], after=after)[0]


def widen_half(w, half):
    rows = w.shape[0] // 2

    def kernel(w_ref, out_ref):
        out_ref[...] = w_ref[half * rows : (half + 1) * rows, :].astype(F32)

    return kernel_call(kernel, [((rows, w.shape[1]), F32)], [w])[0]


def join_halves(keep, recv):
    m, n = keep.shape

    def kernel(keep_ref, low_ref, high_ref, w_ref, t_ref):
        w_ref[:, :n] = keep_ref[...]
        t_ref[:n, :] = keep_ref[...].T
        for i, ref in enumerate((low_ref, high_ref)):
            here = slice(i * m // 2, (i + 1) * m // 2)
            part = ref[...].astype(BF16)
            w_ref[here, n:] = part
            t_ref[n:, here] = part.T

    return kernel_call(kernel, [((m, 2 * n), BF16), ((2 * n, m), BF16)], [keep, *recv])


def join_cols_kernel(keep_ref, recv_ref, w_ref, t_ref):
    n = keep_ref.shape[1]
    recv = recv_ref[...].astype(BF16)
    w_ref[:, :n] = keep_ref[...]
    w_ref[:, n:] = recv
    t_ref[:n, :] = keep_ref[...].T
    t_ref[n:, :] = recv.T


def join_cols(keep, recv, parts=4):
    m, n = keep.shape
    step = m // parts
    shapes = [jax.ShapeDtypeStruct((m, 2 * n), BF16), jax.ShapeDtypeStruct((2 * n, m), BF16)]
    return pl.pallas_call(
        join_cols_kernel,
        grid=(parts,),
        out_shape=shapes,
        in_specs=[pl.BlockSpec((step, n), lambda i: (i, 0))] * 2,
        out_specs=[
            pl.BlockSpec((step, 2 * n), lambda i: (i, 0)),
            pl.BlockSpec((2 * n, step), lambda i: (0, i)),
        ],
        compiler_params=pltpu.CompilerParams(vmem_limit_bytes=12 * 2**20),
        cost_estimate=pl.CostEstimate(
            flops=0,
            transcendentals=0,
            bytes_accessed=sum(map(size_of, [keep, recv, *shapes])),
        ),
    )(keep, recv)


def join_rows_kernel(keep_ref, recv_ref, w_ref):
    n = keep_ref.shape[0]
    w_ref[:n, :] = keep_ref[...]
    w_ref[n:, :] = recv_ref[...].astype(BF16)


def join_rows(keep, recv, parts=4):
    m, n = keep.shape
    step = n // parts
    shape = jax.ShapeDtypeStruct((2 * m, n), BF16)
    return pl.pallas_call(
        join_rows_kernel,
        grid=(parts,),
        out_shape=shape,
        in_specs=[pl.BlockSpec((m, step), lambda i: (0, i))] * 2,
        out_specs=pl.BlockSpec((2 * m, step), lambda i: (0, i)),
        compiler_params=pltpu.CompilerParams(vmem_limit_bytes=12 * 2**20),
        cost_estimate=pl.CostEstimate(
            flops=0,
            transcendentals=0,
            bytes_accessed=sum(map(size_of, [keep, recv, shape])),
        ),
    )(keep, recv)


def forward(deep, w_ref, *refs):
    vec, outs, (rhs_ref, sum_ref) = refs[:-8], refs[-8:-2], refs[-2:]
    own, other = vec[0][...], vec[1][...]
    blocks = own.shape[0]
    if len(vec) == 3:
        own = own - vec[2][:blocks]
        other = other - vec[2][blocks:]
    for i in range(blocks):
        put_split(rhs_ref, i * 128, own[i])
        put_split(rhs_ref, (blocks + i) * 128, other[i])
    step = w_ref.shape[0] // 4
    for i in range(4):
        here = slice(i * step, (i + 1) * step)
        sum_ref[here, :] = product(w_ref[here, :], rhs_ref)
    left = left_lanes((WIDE, 2 * WIDE))
    for colour in range(2):
        send_ref, next_ref, keep_ref = outs[3 * colour : 3 * colour + 3]
        for i, start in enumerate(block_starts(deep, colour)):
            low = sum_ref[pl.ds(start, WIDE), :]
            high = sum_ref[pl.ds(start + WIDE, WIDE), :]
            block = jnp.where(left, low, high)
            if i < 4:
                keep_ref[i] = block
            elif i < 8:
                next_ref[i - 4] = block
            else:
                send_ref[i - 8] = block


def backward(deep, w_ref, near0, far0, near1, far1, *refs):
    outs, rhs_ref = refs[:-1], refs[-1]
    for colour, (near, far) in enumerate(((near0, far0), (near1, far1))):
        for i, start in enumerate(block_starts(deep, colour)):
            put_split(rhs_ref, start, near[i] if i < 8 else far[i - 8])
    total = product(w_ref[...], rhs_ref)
    blocks = outs[0].shape[0]
    for i in range(blocks):
        outs[0][i] = take_block(total, i * 128)
        if len(outs) > 1 and i >= blocks // 2:
            outs[1][i - blocks // 2] = outs[0][i]


def run_forward(w, vec, deep, after=()):
    m, k = w.shape
    return kernel_call(
        functools.partial(forward, deep),
        [((8, WIDE, 128), F32), ((4, WIDE, 128), F32), ((4, WIDE, 128), F32)] * 2,
        [w, *vec],
        [pltpu.VMEM((k, 128), BF16), pltpu.VMEM((m, 128), F32)],
        flops=2 * m * k * 128,
        limit=16,
        after=after,
    )


def run_backward(w, pieces, deep, alone, after=()):
    m, k = w.shape
    blocks = m // 128
    outs = [((blocks, WIDE, 128), F32)]
    if alone:
        outs.append(((blocks // 2, WIDE, 128), F32))
    return kernel_call(
        functools.partial(backward, deep),
        outs,
        [w, *pieces],
        [pltpu.VMEM((k, 128), BF16)],
        flops=2 * m * k * 128,
        limit=16,
        after=after,
    )


def depth_load(value, deep):
    half = value.shape[0] // 2
    value = value[:half] + swap(value[half:], NEAR)
    if deep:
        value = value[:1] + swap(value[1:], FAR)
    return value


def by_core(own):
    c = lax.axis_index("panel") % 2
    mine = jnp.where(c == 0, own[:, 0], own[:, 1])
    theirs = jnp.where(c == 0, own[:, 1], own[:, 0])
    return [mine, swap(theirs, CORE)]


def plane_sum(parts):
    out = []
    firsts = [swap_first(parts[3 * k], k) for k in range(2)]
    for k in range(2):
        (follow,) = glue(lambda a, b: (a + b[4:],), parts[3 * k + 1], firsts[k])
        out += [parts[3 * k + 2], firsts[k], swap_second(follow, k)]
    return out


def colours(k0, f0, s0, k1, f1, s1):
    return jnp.stack([k0 + f0[:4] + s0, k1 + f1[:4] + s1], 1)


def depth_total(pieces, deep):
    if not deep:

        def both(*p):
            v = colours(*p)
            return v, jnp.concatenate([v[2:], v[:2]], 0)

        value, turned = glue(both, *pieces)
        got = swap(turned, NEAR)
        return glue(lambda v, g: ((v + g)[:, 0], (v + g)[:, 1]), value, got), [got]

    def halves(*p):
        v = colours(*p)
        return v[:2], v[2:]

    keep, send = glue(halves, *pieces)

    def turn(k, g):
        v = k + g
        return v, jnp.concatenate([v[1:], v[:1]], 0)

    near = swap(send, NEAR)
    keep, turned = glue(turn, keep, near)
    far = swap(turned, FAR)
    (pair,) = glue(lambda k, g: (k + g,), keep, far)
    return lines(pair), [near, far]


def lines(pair, after=()):
    def put(p, g):
        return tuple(jnp.concatenate([p[:, k], g[:, k]], 0) for k in range(2))

    return glue(put, pair, swap(pair, NEAR), after=after)


def plane_spread(pair_of_lines):
    pieces = []
    seconds = [swap_second(line, k) for k, line in enumerate(pair_of_lines)]
    for k, line in enumerate(pair_of_lines):
        (near,) = glue(lambda a, b: (jnp.concatenate([a, b], 0),), line, seconds[k])
        pieces += [near, swap_first(near, k)]
    return pieces


def unpack_kernel(mine_ref, recv_ref, out_ref):
    c = lax.axis_index("panel") % 2
    blocks = recv_ref.shape[0]
    left = left_lanes((WIDE, 128))
    for i in range(blocks):
        mine, recv = mine_ref[i], recv_ref[i]
        here = jnp.broadcast_to(c == 0, mine.shape)
        p0, p1 = jnp.where(here, mine, recv), jnp.where(here, recv, mine)
        out_ref[i * 128 : i * 128 + WIDE, :] = jnp.where(left, p0, pltpu.roll(p1, WIDE, 1))
        out_ref[i * 128 + WIDE : (i + 1) * 128, :] = jnp.where(left, pltpu.roll(p0, WIDE, 1), p1)


def unpack(mine, recv):
    return kernel_call(unpack_kernel, [((recv.shape[0] * 128, 128), F32)], [mine, recv])[0]


def fast_body(border, solution, winv_top, winv_mid, coupling):
    ready = kernel_call(
        prep_top, [((32, 1152), F32)] * 4, [border[0], solution[0]]
    )
    tops = plane_inputs(ready)
    top_w, top_t = join_halves(winv_top, [swap(widen_half(winv_top, i), CORE) for i in range(2)])
    keep, send, sol_all = kernel_call(
        top_load_kernel,
        [((4, 2, WIDE, 128), F32)] * 2 + [((128, 128), BF16)],
        tops,
        [pltpu.VMEM((128, 1024), BF16)],
        flops=2 * 128 * 1024 * 128,
    )
    got = swap_loads(send)
    load = by_core(depth_load(keep + got, True))

    mids = plane_inputs(
        kernel_call(prep_mid, [((32, 1024), F32)] * 4, [border[0]], after=[got])
    )

    parts = run_forward(top_w, load, True, after=mids)
    line, marks = depth_total(plane_sum(parts), True)
    cou_w = join_rows(coupling, swap(widen(coupling, after=marks[:1]), CORE))
    mid_w, mid_t = join_cols(winv_mid, swap(widen(winv_mid, after=marks[:1]), CORE))
    pieces = plane_spread(line)
    adjoint, theirs = run_backward(top_t, pieces, True, True)
    top_out = unpack(adjoint, swap(theirs, CORE))

    keep, send = kernel_call(
        mid_load_kernel,
        [((4, 2, WIDE, 128), F32)] * 2,
        [*mids, sol_all],
        [pltpu.VMEM((128, 1024), BF16)],
        flops=2 * 128 * 1024 * 128,
    )
    load = by_core(depth_load(keep + swap_loads(send), False))

    (pair,) = glue(lambda a, b: (jnp.stack([a, b]),), adjoint, swap(adjoint, FAR))
    pieces = plane_spread(lines(pair))
    (part,) = run_backward(cou_w, pieces, True, False)
    parts = run_forward(mid_w, [*load, part], False)
    pieces = plane_spread(depth_total(plane_sum(parts), False)[0])
    adjoint, theirs = run_backward(mid_t, pieces, False, True)
    return top_out, unpack(adjoint, swap(theirs, CORE))


def solution(mesh):
    placed = (
        P("leaf", "panel", None),
        P("leaf", "panel", None),
        P(None, AXES),
        P(None, AXES),
        P(AXES, None),
    )
    fits = mesh.shape["leaf"] == 8 and mesh.shape["panel"] == 4
    return jax.shard_map(
        fast_body if fits else plain_body,
        mesh=mesh,
        in_specs=placed,
        out_specs=(P(AXES, None), P(AXES, None)),
        check_vma=False,
    )
```

profile of v0, /device:TPU:0, one launch (start us, length us, event | category | flops | bytes accessed | tf_op | source)
XLA Modules:
  0.0 149.0 jit_solution(12974738989470486395)
XLA Ops:
  3.1 2.6 %collective-permute-start.3 = (f32[32,1152]{1,0:T(8,128)S(1)}, f32[32,1152]{1,0:T(8,128)S(1)}, u32[]{:S(2)}, u32[]{:S(2)}) collective-permute-start(f32[32,1152]{1,0:T(8,128)S(1)} %get-tuple-element.51), channel_id=1, source_target_pairs={{0,2},{1,5},{2,0},{3,7},{4,6},{5,1},{6,4},{7,3},{8,10},{9,13},{10,... | collective-permute-start | bytes 442376 | tf_op jit(solution)/shard_map/ppermute | solution.py:53
  5.7 3.6 %collective-permute-done.3.refs_2_ = f32[32,1152]{1,0:T(8,128)S(1)} collective-permute-done((f32[32,1152]{1,0:T(8,128)S(1)}, f32[32,1152]{1,0:T(8,128)S(1)}, u32[]{:S(2)}, u32[]{:S(2)}) %collective-permute-start.3) | collective-permute-done | bytes 147488 | tf_op jit(solution)/shard_map/ppermute | solution.py:53
  10.9 2.1 %collective-permute-start.5 = (f32[4,2,64,128]{3,2,1,0:T(8,128)S(1)}, f32[4,2,64,128]{3,2,1,0:T(8,128)S(1)}, u32[]{:S(2)}, u32[]{:S(2)}) collective-permute-start(f32[4,2,64,128]{3,2,1,0:T(8,128)S(1)} %get-tuple-element.54), channel_id=1, source_target_pairs={{0,4},{1,3},{2,6},{3,1},{4,0},{5,7},{6,2},{7,5},{8,12},{9,11},{10,... | collective-permute-start | bytes 786440 | tf_op jit(solution)/shard_map/ppermute | solution.py:53
  13.0 1.2 copy-done
  17.4 2.1 %collective-permute-start.6 = (f32[2,2,64,128]{3,2,1,0:T(8,128)S(1)}, f32[2,2,64,128]{3,2,1,0:T(8,128)S(1)}, u32[]{:S(2)}, u32[]{:S(2)}) collective-permute-start(f32[2,2,64,128]{3,2,1,0:T(8,128)S(1)} %slice.45), channel_id=1, source_target_pairs={{0,8},{1,9},{2,10},{3,11},{4,12},{5,13},{6,14},{7,15},{8,0},{9,1},... | collective-permute-start | bytes 393224 | tf_op jit(solution)/shard_map/ppermute | solution.py:53
  19.6 2.9 %collective-permute-done.6 = f32[2,2,64,128]{3,2,1,0:T(8,128)S(1)} collective-permute-done((f32[2,2,64,128]{3,2,1,0:T(8,128)S(1)}, f32[2,2,64,128]{3,2,1,0:T(8,128)S(1)}, u32[]{:S(2)}, u32[]{:S(2)}) %collective-permute-start.6) | collective-permute-done | bytes 131104 | tf_op jit(solution)/shard_map/ppermute | solution.py:53
  22.6 3.1 %collective-permute-start.7 = (f32[1,2,64,128]{3,2,1,0:T(8,128)S(1)}, f32[1,2,64,128]{3,2,1,0:T(8,128)S(1)}, u32[]{:S(2)}, u32[]{:S(2)}) collective-permute-start(f32[1,2,64,128]{3,2,1,0:T(8,128)S(1)} %slice.47), channel_id=1, source_target_pairs={{0,16},{1,17},{2,18},{3,19},{4,20},{5,21},{6,22},{7,23},{8,24},{9,... | collective-permute-start | bytes 196616 | tf_op jit(solution)/shard_map/ppermute | solution.py:53
  25.7 1.5 %collective-permute-start.10 = (f32[32,1024]{1,0:T(8,128)S(1)}, f32[32,1024]{1,0:T(8,128)S(1)}, u32[]{:S(2)}, u32[]{:S(2)}) collective-permute-start(f32[32,1024]{1,0:T(8,128)S(1)} %get-tuple-element.57), channel_id=1, source_target_pairs={{0,2},{1,5},{2,0},{3,7},{4,6},{5,1},{6,4},{7,3},{8,10},{9,13},{10,... | collective-permute-start | bytes 393224 | tf_op jit(solution)/shard_map/ppermute | solution.py:53
  28.5 2.0 %shard_map.70 = (bf16[4096,256]{1,0:T(8,128)(2,1)S(1)}, bf16[256,4096]{1,0:T(8,128)(2,1)S(1)}) custom-call(bf16[4096,128]{1,0:T(8,128)(2,1)S(1)} %copy-done.1, f32[2048,128]{1,0:T(8,128)S(1)} %collective-permute-done.refs_1_, f32[2048,128]{1,0:T(8,128)} %collective-permute-done.1.refs_2_), custom_call_target="tpu_custom_call" | custom-call | bytes 7340032 | tf_op jit(solution)/shard_map/pallas_call | solution.py:118
  33.2 1.6 %collective-permute-start.14 = (f32[8,64,128]{2,1,0:T(8,128)S(1)}, f32[8,64,128]{2,1,0:T(8,128)S(1)}, u32[]{:S(2)}, u32[]{:S(2)}) collective-permute-start(f32[8,64,128]{2,1,0:T(8,128)S(1)} %get-tuple-element.63), channel_id=1, source_target_pairs={{0,4},{1,5},{2,6},{3,7},{4,0},{5,1},{6,2},{7,3},{8,12},{9,13},{10,... | collective-permute-start | bytes 786440 | tf_op jit(solution)/shard_map/ppermute | solution.py:53
  34.7 1.5 collective-permute-start.12
  36.2 4.9 %collective-permute-done.14.refs_1_.refs_4_ = f32[8,64,128]{2,1,0:T(8,128)S(1)} collective-permute-done((f32[8,64,128]{2,1,0:T(8,128)S(1)}, f32[8,64,128]{2,1,0:T(8,128)S(1)}, u32[]{:S(2)}, u32[]{:S(2)}) %collective-permute-start.14) | collective-permute-done | bytes 262176 | tf_op jit(solution)/shard_map/ppermute | solution.py:53
  41.8 1.6 %collective-permute-start.13 = (f32[4,64,128]{2,1,0:T(8,128)S(1)}, f32[4,64,128]{2,1,0:T(8,128)S(1)}, u32[]{:S(2)}, u32[]{:S(2)}) collective-permute-start(f32[4,64,128]{2,1,0:T(8,128)S(1)} %shard_map.75), channel_id=1, source_target_pairs={{0,4},{1,5},{2,6},{3,7},{4,0},{5,1},{6,2},{7,3},{8,12},{9,13},{10,... | collective-permute-start | bytes 393224 | tf_op jit(solution)/shard_map/ppermute | solution.py:53
  43.4 2.8 %collective-permute-done.15.refs_5_ = f32[4,64,128]{2,1,0:T(8,128)S(1)} collective-permute-done((f32[4,64,128]{2,1,0:T(8,128)S(1)}, f32[4,64,128]{2,1,0:T(8,128)S(1)}, u32[]{:S(2)}, u32[]{:S(2)}) %collective-permute-start.15) | collective-permute-done | bytes 131104 | tf_op jit(solution)/shard_map/ppermute | solution.py:53
  46.9 1.7 %collective-permute-start.16 = (f32[2,2,64,128]{3,2,1,0:T(8,128)S(1)}, f32[2,2,64,128]{3,2,1,0:T(8,128)S(1)}, u32[]{:S(2)}, u32[]{:S(2)}) collective-permute-start(f32[2,2,64,128]{3,2,1,0:T(8,128)S(1)} %get-tuple-element.66), channel_id=1, source_target_pairs={{0,8},{1,9},{2,10},{3,11},{4,12},{5,13},{6,14},{7,15},{8,0},{9,1},... | collective-permute-start | bytes 393224 | tf_op jit(solution)/shard_map/ppermute | solution.py:53
  48.5 3.4 %collective-permute-done.16.refs_1_ = f32[2,2,64,128]{3,2,1,0:T(8,128)S(1)} collective-permute-done((f32[2,2,64,128]{3,2,1,0:T(8,128)S(1)}, f32[2,2,64,128]{3,2,1,0:T(8,128)S(1)}, u32[]{:S(2)}, u32[]{:S(2)}) %collective-permute-start.16) | collective-permute-done | bytes 131104 | tf_op jit(solution)/shard_map/ppermute | solution.py:53
  53.1 2.8 %collective-permute-start.17 = (f32[2,2,64,128]{3,2,1,0:T(8,128)S(1)}, f32[2,2,64,128]{3,2,1,0:T(8,128)S(1)}, u32[]{:S(2)}, u32[]{:S(2)}) collective-permute-start(f32[2,2,64,128]{3,2,1,0:T(8,128)S(1)} %get-tuple-element.68), channel_id=1, source_target_pairs={{0,16},{1,17},{2,18},{3,19},{4,20},{5,21},{6,22},{7,23},{8,24},{9,... | collective-permute-start | bytes 393224 | tf_op jit(solution)/shard_map/ppermute | solution.py:53
  55.9 6.5 %collective-permute-done.17.refs_1_ = f32[2,2,64,128]{3,2,1,0:T(8,128)S(1)} collective-permute-done((f32[2,2,64,128]{3,2,1,0:T(8,128)S(1)}, f32[2,2,64,128]{3,2,1,0:T(8,128)S(1)}, u32[]{:S(2)}, u32[]{:S(2)}) %collective-permute-start.17) | collective-permute-done | bytes 131104 | tf_op jit(solution)/shard_map/ppermute | solution.py:53
  63.2 4.2 %collective-permute-done.18.refs_1_ = f32[2,2,64,128]{3,2,1,0:T(8,128)S(1)} collective-permute-done((f32[2,2,64,128]{3,2,1,0:T(8,128)S(1)}, f32[2,2,64,128]{3,2,1,0:T(8,128)S(1)}, u32[]{:S(2)}, u32[]{:S(2)}) %collective-permute-start.18) | collective-permute-done | bytes 131104 | tf_op jit(solution)/shard_map/ppermute | solution.py:53
  67.5 1.4 collective-permute-start.21
  69.8 2.7 %collective-permute-done.21.refs_1_ = f32[4,64,128]{2,1,0:T(8,128)S(1)} collective-permute-done((f32[4,64,128]{2,1,0:T(8,128)S(1)}, f32[4,64,128]{2,1,0:T(8,128)S(1)}, u32[]{:S(2)}, u32[]{:S(2)}) %collective-permute-start.21) | collective-permute-done | bytes 131104 | tf_op jit(solution)/shard_map/ppermute | solution.py:53
  72.6 1.6 %collective-permute-start.22 = (f32[8,64,128]{2,1,0:T(8,128)S(1)}, f32[8,64,128]{2,1,0:T(8,128)S(1)}, u32[]{:S(2)}, u32[]{:S(2)}) collective-permute-start(f32[8,64,128]{2,1,0:T(8,128)S(1)} %shard_map.82.refs_3_), channel_id=1, source_target_pairs={{0,4},{1,5},{2,6},{3,7},{4,0},{5,1},{6,2},{7,3},{8,12},{9,13},{10,... | collective-permute-start | bytes 786440 | tf_op jit(solution)/shard_map/ppermute | solution.py:53
  76.4 1.8 %collective-permute-start.25 = (f32[4,2,64,128]{3,2,0,1:T(8,128)S(1)}, f32[4,2,64,128]{3,2,0,1:T(8,128)S(1)}, u32[]{:S(2)}, u32[]{:S(2)}) collective-permute-start(f32[4,2,64,128]{3,2,0,1:T(8,128)S(1)} %copy.7), channel_id=1, source_target_pairs={{0,4},{1,3},{2,6},{3,1},{4,0},{5,7},{6,2},{7,5},{8,12},{9,11},{10,... | collective-permute-start | bytes 786440 | tf_op jit(solution)/shard_map/ppermute | solution.py:53
  79.3 2.7 %collective-permute-done.20.refs_2_ = f32[8,64,128]{2,1,0:T(8,128)S(1)} collective-permute-done((f32[8,64,128]{2,1,0:T(8,128)S(1)}, f32[8,64,128]{2,1,0:T(8,128)S(1)}, u32[]{:S(2)}, u32[]{:S(2)}) %collective-permute-start.20) | collective-permute-done | bytes 262176 | tf_op jit(solution)/shard_map/ppermute | solution.py:53
  82.0 1.2 shard_map.83
  83.2 4.2 %collective-permute-start.29 = (f32[2,64,128]{2,1,0:T(8,128)S(1)}, f32[2,64,128]{2,1,0:T(8,128)S(1)}, u32[]{:S(2)}, u32[]{:S(2)}) collective-permute-start(f32[2,64,128]{2,1,0:T(8,128)S(1)} %get-tuple-element.71.refs_0_), channel_id=1, source_target_pairs={{0,16},{1,17},{2,18},{3,19},{4,20},{5,21},{6,22},{7,23},{8,24},{9,... | collective-permute-start | bytes 196616 | tf_op jit(solution)/shard_map/ppermute | solution.py:53
  87.4 2.2 %collective-permute-done.29.refs_1_ = f32[2,64,128]{2,1,0:T(8,128)S(1)} collective-permute-done((f32[2,64,128]{2,1,0:T(8,128)S(1)}, f32[2,64,128]{2,1,0:T(8,128)S(1)}, u32[]{:S(2)}, u32[]{:S(2)}) %collective-permute-start.29) | collective-permute-done | bytes 65568 | tf_op jit(solution)/shard_map/ppermute | solution.py:53
  89.7 1.8 %collective-permute-start.30 = (f32[2,2,64,128]{3,2,1,0:T(8,128)S(1)}, f32[2,2,64,128]{3,2,1,0:T(8,128)S(1)}, u32[]{:S(2)}, u32[]{:S(2)}) collective-permute-start(f32[2,2,64,128]{3,2,1,0:T(8,128)S(1)} %shard_map.90.refs_0_), channel_id=1, source_target_pairs={{0,8},{1,9},{2,10},{3,11},{4,12},{5,13},{6,14},{7,15},{8,0},{9,1},... | collective-permute-start | bytes 393224 | tf_op jit(solution)/shard_map/ppermute | solution.py:53
  91.4 3.3 %collective-permute-done.30.refs_1_ = f32[2,2,64,128]{3,2,1,0:T(8,128)S(1)} collective-permute-done((f32[2,2,64,128]{3,2,1,0:T(8,128)S(1)}, f32[2,2,64,128]{3,2,1,0:T(8,128)S(1)}, u32[]{:S(2)}, u32[]{:S(2)}) %collective-permute-start.30) | collective-permute-done | bytes 131104 | tf_op jit(solution)/shard_map/ppermute | solution.py:53
  94.7 1.2 collective-permute-start.33
  97.1 1.8 %collective-permute-start.26 = (f32[2,2,64,128]{3,2,0,1:T(8,128)S(1)}, f32[2,2,64,128]{3,2,0,1:T(8,128)S(1)}, u32[]{:S(2)}, u32[]{:S(2)}) collective-permute-start(f32[2,2,64,128]{3,2,0,1:T(8,128)S(1)} %slice.51), channel_id=1, source_target_pairs={{0,8},{1,9},{2,10},{3,11},{4,12},{5,13},{6,14},{7,15},{8,0},{9,1},... | collective-permute-start | bytes 393224 | tf_op jit(solution)/shard_map/ppermute | solution.py:53
  100.9 1.3 collective-permute-start.32
  103.4 1.8 %shard_map.86 = (bf16[4096,512]{1,0:T(8,128)(2,1)S(1)}, bf16[512,4096]{1,0:T(8,128)(2,1)S(1)}) custom-call(bf16[4096,256]{1,0:T(8,128)(2,1)S(1)} %copy-done.3, f32[4096,256]{1,0:T(8,128)S(1)} %collective-permute-done.24.recv_ref), custom_call_target="tpu_custom_call" | custom-call | bytes 14680064 | tf_op jit(solution)/shard_map/pallas_call | solution.py:294
  106.2 1.1 collective-permute-done.32.refs_2_
  107.3 1.7 %shard_map.94.refs_3_ = f32[4,64,128]{2,1,0:T(8,128)S(1)} custom-call(bf16[512,4096]{1,0:T(8,128)(2,1)S(1)} %shard_map.89.refs_0_, f32[8,64,128]{2,1,0:T(8,128)S(1)} %shard_map.92.refs_1_, f32[8,64,128]{2,1,0:T(8,128)S(1)} %collective-permute-done.32.refs_2_, f32[8,64,128]{2,1,0:T(8,128)S(1)} %shard_map.93.refs_3_, ...), custom_call_target="tpu_custom_call" | custom-call | flops 536870912 | bytes 5373952 | tf_op jit(solution)/shard_map/pallas_call | solution.py:118
  109.1 1.5 %shard_map.95 = (f32[8,64,128]{2,1,0:T(8,128)S(1)}, f32[4,64,128]{2,1,0:T(8,128)S(1)}, f32[4,64,128]{2,1,0:T(8,128)S(1)}, f32[8,64,128]{2,1,0:T(8,128)S(1)}, f32...) custom-call(bf16[4096,512]{1,0:T(8,128)(2,1)S(1)} %get-tuple-element.74.refs_0_, ...), custom_call_target="tpu_custom_call" | custom-call | flops 536870912 | bytes 5505024 | tf_op jit(solution)/shard_map/pallas_call | solution.py:118
  110.6 1.2 collective-permute-start.37
  112.8 4.5 %collective-permute-done.37.refs_1_.refs_4_ = f32[8,64,128]{2,1,0:T(8,128)S(1)} collective-permute-done((f32[8,64,128]{2,1,0:T(8,128)S(1)}, f32[8,64,128]{2,1,0:T(8,128)S(1)}, u32[]{:S(2)}, u32[]{:S(2)}) %collective-permute-start.37) | collective-permute-done | bytes 262176 | tf_op jit(solution)/shard_map/ppermute | solution.py:53
  118.8 1.2 collective-permute-start.36
  120.0 2.4 %collective-permute-done.38.refs_5_ = f32[4,64,128]{2,1,0:T(8,128)S(1)} collective-permute-done((f32[4,64,128]{2,1,0:T(8,128)S(1)}, f32[4,64,128]{2,1,0:T(8,128)S(1)}, u32[]{:S(2)}, u32[]{:S(2)}) %collective-permute-start.38) | collective-permute-done | bytes 131104 | tf_op jit(solution)/shard_map/ppermute | solution.py:53
  122.4 1.5 collective-permute-done.36.refs_2_
  123.9 1.3 collective-permute-start.39
  125.2 5.1 %collective-permute-done.39.refs_1_ = f32[4,2,64,128]{3,2,1,0:T(8,128)S(1)} collective-permute-done((f32[4,2,64,128]{3,2,1,0:T(8,128)S(1)}, f32[4,2,64,128]{3,2,1,0:T(8,128)S(1)}, u32[]{:S(2)}, u32[]{:S(2)}) %collective-permute-start.39) | collective-permute-done | bytes 262176 | tf_op jit(solution)/shard_map/ppermute | solution.py:53
  130.4 1.7 %collective-permute-start.42 = (f32[4,64,128]{2,1,0:T(8,128)S(1)}, f32[4,64,128]{2,1,0:T(8,128)S(1)}, u32[]{:S(2)}, u32[]{:S(2)}) collective-permute-start(f32[4,64,128]{2,1,0:T(8,128)S(1)} %get-tuple-element.89.refs_0_), channel_id=1, source_target_pairs={{0,2},{1,3},{2,0},{3,1},{4,6},{5,7},{6,4},{7,5},{8,10},{9,11},{10,... | collective-permute-start | bytes 393224 | tf_op jit(solution)/shard_map/ppermute | solution.py:53
  133.2 3.6 %collective-permute-done.42.refs_1_ = f32[4,64,128]{2,1,0:T(8,128)S(1)} collective-permute-done((f32[4,64,128]{2,1,0:T(8,128)S(1)}, f32[4,64,128]{2,1,0:T(8,128)S(1)}, u32[]{:S(2)}, u32[]{:S(2)}) %collective-permute-start.42) | collective-permute-done | bytes 131104 | tf_op jit(solution)/shard_map/ppermute | solution.py:53
  137.9 1.4 collective-permute-start.41
  139.4 3.9 %collective-permute-done.43.refs_4_ = f32[8,64,128]{2,1,0:T(8,128)S(1)} collective-permute-done((f32[8,64,128]{2,1,0:T(8,128)S(1)}, f32[8,64,128]{2,1,0:T(8,128)S(1)}, u32[]{:S(2)}, u32[]{:S(2)}) %collective-permute-start.43) | collective-permute-done | bytes 262176 | tf_op jit(solution)/shard_map/ppermute | solution.py:53
  144.4 1.7 %shard_map.102 = (f32[4,64,128]{2,1,0:T(8,128)S(1)}, f32[2,64,128]{2,1,0:T(8,128)S(1)}) custom-call(bf16[512,4096]{1,0:T(8,128)(2,1)S(1)} %get-tuple-element.73.refs_0_, f32[8,64,128]{2,1,0:T(8,128)S(1)} %shard_map.100.refs_1_, f32[8,64,128]{2,1,0:T(8,128)S(1)} %collective-permute-done.41.refs_2_, f32[8,64,128]{2,1,0:T(8,128)S(1)} %shard_map.101.refs_3_, ...), custom_call_target="tpu_custom_call" | custom-call | flops 536870912 | bytes 5439488 | tf_op jit(solution)/shard_map/pallas_call | solution.py:118
  (103 shorter events, 33.0 us)
Async XLA Ops:
  0.6 27.9 %copy-start.1 = (bf16[4096,128]{1,0:T(8,128)(2,1)S(1)}, bf16[4096,128]{1,0:T(8,128)(2,1)}, u32[]{:S(2)}) copy-start(bf16[4096,128]{1,0:T(8,128)(2,1)} %refs_0_.7) | copy-start | bytes 3145732
  2.6 3.2 %collective-permute-start.2 = (f32[32,1152]{1,0:T(8,128)S(1)}, f32[32,1152]{1,0:T(8,128)S(1)}, u32[]{:S(2)}, u32[]{:S(2)}) collective-permute-start(f32[32,1152]{1,0:T(8,128)S(1)} %get-tuple-element.50), channel_id=1, source_target_pairs={{0,1},{1,0},{2,3},{3,2},{4,5},{5,4},{6,7},{7,6},{8,9},{9,8},{10,11... | collective-permute-start | bytes 442376 | tf_op jit(solution)/shard_map/ppermute | solution.py:53
  3.1 6.3 %collective-permute-start.3 = (f32[32,1152]{1,0:T(8,128)S(1)}, f32[32,1152]{1,0:T(8,128)S(1)}, u32[]{:S(2)}, u32[]{:S(2)}) collective-permute-start(f32[32,1152]{1,0:T(8,128)S(1)} %get-tuple-element.51), channel_id=1, source_target_pairs={{0,2},{1,5},{2,0},{3,7},{4,6},{5,1},{6,4},{7,3},{8,10},{9,13},{10,... | collective-permute-start | bytes 442376 | tf_op jit(solution)/shard_map/ppermute | solution.py:53
  5.6 4.7 %collective-permute-start.4 = (f32[32,1152]{1,0:T(8,128)S(1)}, f32[32,1152]{1,0:T(8,128)S(1)}, u32[]{:S(2)}, u32[]{:S(2)}) collective-permute-start(f32[32,1152]{1,0:T(8,128)S(1)} %get-tuple-element.52), channel_id=1, source_target_pairs={{0,5},{1,2},{2,7},{3,0},{4,1},{5,6},{6,3},{7,4},{8,13},{9,10},{10,... | collective-permute-start | bytes 442376 | tf_op jit(solution)/shard_map/ppermute | solution.py:53
  10.9 6.5 %collective-permute-start.5 = (f32[4,2,64,128]{3,2,1,0:T(8,128)S(1)}, f32[4,2,64,128]{3,2,1,0:T(8,128)S(1)}, u32[]{:S(2)}, u32[]{:S(2)}) collective-permute-start(f32[4,2,64,128]{3,2,1,0:T(8,128)S(1)} %get-tuple-element.54), channel_id=1, source_target_pairs={{0,4},{1,3},{2,6},{3,1},{4,0},{5,7},{6,2},{7,5},{8,12},{9,11},{10,... | collective-permute-start | bytes 786440 | tf_op jit(solution)/shard_map/ppermute | solution.py:53
  14.3 11.4 %copy-start.5 = (bf16[1,32,8192]{2,1,0:T(8,128)(2,1)S(1)}, bf16[1,32,8192]{2,1,0:T(8,128)(2,1)}, u32[]{:S(2)}) copy-start(bf16[1,32,8192]{2,1,0:T(8,128)(2,1)} %param.5) | copy-start | bytes 1572868
  15.4 12.6 %collective-permute-start = (f32[2048,128]{1,0:T(8,128)}, f32[2048,128]{1,0:T(8,128)S(1)}, u32[]{:S(2)}, u32[]{:S(2)}) collective-permute-start(f32[2048,128]{1,0:T(8,128)} %shard_map.68), channel_id=1, source_target_pairs={{0,1},{1,0},{2,3},{3,2},{4,5},{5,4},{6,7},{7,6},{8,9},{9,8},{10,11... | collective-permute-start | bytes 3145736 | tf_op jit(solution)/shard_map/ppermute | solution.py:53
  16.4 12.1 %collective-permute-start.1 = (f32[2048,128]{1,0:T(8,128)}, f32[2048,128]{1,0:T(8,128)}, u32[]{:S(2)}, u32[]{:S(2)}) collective-permute-start(f32[2048,128]{1,0:T(8,128)} %shard_map.69), channel_id=1, source_target_pairs={{0,1},{1,0},{2,3},{3,2},{4,5},{5,4},{6,7},{7,6},{8,9},{9,8},{10,11... | collective-permute-start | bytes 3145736 | tf_op jit(solution)/shard_map/ppermute | solution.py:53
  17.4 5.1 %collective-permute-start.6 = (f32[2,2,64,128]{3,2,1,0:T(8,128)S(1)}, f32[2,2,64,128]{3,2,1,0:T(8,128)S(1)}, u32[]{:S(2)}, u32[]{:S(2)}) collective-permute-start(f32[2,2,64,128]{3,2,1,0:T(8,128)S(1)} %slice.45), channel_id=1, source_target_pairs={{0,8},{1,9},{2,10},{3,11},{4,12},{5,13},{6,14},{7,15},{8,0},{9,1},... | collective-permute-start | bytes 393224 | tf_op jit(solution)/shard_map/ppermute | solution.py:53
  22.6 5.3 %collective-permute-start.7 = (f32[1,2,64,128]{3,2,1,0:T(8,128)S(1)}, f32[1,2,64,128]{3,2,1,0:T(8,128)S(1)}, u32[]{:S(2)}, u32[]{:S(2)}) collective-permute-start(f32[1,2,64,128]{3,2,1,0:T(8,128)S(1)} %slice.47), channel_id=1, source_target_pairs={{0,16},{1,17},{2,18},{3,19},{4,20},{5,21},{6,22},{7,23},{8,24},{9,... | collective-permute-start | bytes 196616 | tf_op jit(solution)/shard_map/ppermute | solution.py:53
  25.7 26.2 %copy-start.2 = (bf16[256,4096]{1,0:T(8,128)(2,1)S(1)}, bf16[256,4096]{1,0:T(8,128)(2,1)}, u32[]{:S(2)}) copy-start(bf16[256,4096]{1,0:T(8,128)(2,1)} %keep_ref.3) | copy-start | bytes 6291460
  25.7 5.6 %collective-permute-start.10 = (f32[32,1024]{1,0:T(8,128)S(1)}, f32[32,1024]{1,0:T(8,128)S(1)}, u32[]{:S(2)}, u32[]{:S(2)}) collective-permute-start(f32[32,1024]{1,0:T(8,128)S(1)} %get-tuple-element.57), channel_id=1, source_target_pairs={{0,2},{1,5},{2,0},{3,7},{4,6},{5,1},{6,4},{7,3},{8,10},{9,13},{10,... | collective-permute-start | bytes 393224 | tf_op jit(solution)/shard_map/ppermute | solution.py:53
  27.2 4.9 %collective-permute-start.11 = (f32[32,1024]{1,0:T(8,128)S(1)}, f32[32,1024]{1,0:T(8,128)S(1)}, u32[]{:S(2)}, u32[]{:S(2)}) collective-permute-start(f32[32,1024]{1,0:T(8,128)S(1)} %get-tuple-element.58), channel_id=1, source_target_pairs={{0,5},{1,2},{2,7},{3,0},{4,1},{5,6},{6,3},{7,4},{8,13},{9,10},{10,... | collective-permute-start | bytes 393224 | tf_op jit(solution)/shard_map/ppermute | solution.py:53
  27.9 4.3 %collective-permute-start.9 = (f32[32,1024]{1,0:T(8,128)S(1)}, f32[32,1024]{1,0:T(8,128)S(1)}, u32[]{:S(2)}, u32[]{:S(2)}) collective-permute-start(f32[32,1024]{1,0:T(8,128)S(1)} %get-tuple-element.56), channel_id=1, source_target_pairs={{0,1},{1,0},{2,3},{3,2},{4,5},{5,4},{6,7},{7,6},{8,9},{9,8},{10,11... | collective-permute-start | bytes 393224 | tf_op jit(solution)/shard_map/ppermute | solution.py:53
  28.0 4.2 %collective-permute-start.8 = (f32[1,64,128]{2,1,0:T(8,128)S(1)}, f32[1,64,128]{2,1,0:T(8,128)S(1)}, u32[]{:S(2)}, u32[]{:S(2)}) collective-permute-start(f32[1,64,128]{2,1,0:T(8,128)S(1)} %get-tuple-element.94), channel_id=1, source_target_pairs={{0,1},{1,0},{2,3},{3,2},{4,5},{5,4},{6,7},{7,6},{8,9},{9,8},{10,11... | collective-permute-start | bytes 98312 | tf_op jit(solution)/shard_map/ppermute | solution.py:53
  33.2 7.9 %collective-permute-start.14 = (f32[8,64,128]{2,1,0:T(8,128)S(1)}, f32[8,64,128]{2,1,0:T(8,128)S(1)}, u32[]{:S(2)}, u32[]{:S(2)}) collective-permute-start(f32[8,64,128]{2,1,0:T(8,128)S(1)} %get-tuple-element.63), channel_id=1, source_target_pairs={{0,4},{1,5},{2,6},{3,7},{4,0},{5,1},{6,2},{7,3},{8,12},{9,13},{10,... | collective-permute-start | bytes 786440 | tf_op jit(solution)/shard_map/ppermute | solution.py:53
  34.7 7.0 %collective-permute-start.12 = (f32[8,64,128]{2,1,0:T(8,128)S(1)}, f32[8,64,128]{2,1,0:T(8,128)S(1)}, u32[]{:S(2)}, u32[]{:S(2)}) collective-permute-start(f32[8,64,128]{2,1,0:T(8,128)S(1)} %get-tuple-element.60), channel_id=1, source_target_pairs={{0,2},{1,3},{2,0},{3,1},{4,6},{5,7},{6,4},{7,5},{8,10},{9,11},{10,... | collective-permute-start | bytes 786440 | tf_op jit(solution)/shard_map/ppermute | solution.py:53
  41.1 5.0 %collective-permute-start.15 = (f32[4,64,128]{2,1,0:T(8,128)S(1)}, f32[4,64,128]{2,1,0:T(8,128)S(1)}, u32[]{:S(2)}, u32[]{:S(2)}) collective-permute-start(f32[4,64,128]{2,1,0:T(8,128)S(1)} %shard_map.76), channel_id=1, source_target_pairs={{0,2},{1,3},{2,0},{3,1},{4,6},{5,7},{6,4},{7,5},{8,10},{9,11},{10,... | collective-permute-start | bytes 393224 | tf_op jit(solution)/shard_map/ppermute | solution.py:53
  41.8 5.0 %collective-permute-start.13 = (f32[4,64,128]{2,1,0:T(8,128)S(1)}, f32[4,64,128]{2,1,0:T(8,128)S(1)}, u32[]{:S(2)}, u32[]{:S(2)}) collective-permute-start(f32[4,64,128]{2,1,0:T(8,128)S(1)} %shard_map.75), channel_id=1, source_target_pairs={{0,4},{1,5},{2,6},{3,7},{4,0},{5,1},{6,2},{7,3},{8,12},{9,13},{10,... | collective-permute-start | bytes 393224 | tf_op jit(solution)/shard_map/ppermute | solution.py:53
  46.9 5.0 %collective-permute-start.16 = (f32[2,2,64,128]{3,2,1,0:T(8,128)S(1)}, f32[2,2,64,128]{3,2,1,0:T(8,128)S(1)}, u32[]{:S(2)}, u32[]{:S(2)}) collective-permute-start(f32[2,2,64,128]{3,2,1,0:T(8,128)S(1)} %get-tuple-element.66), channel_id=1, source_target_pairs={{0,8},{1,9},{2,10},{3,11},{4,12},{5,13},{6,14},{7,15},{8,0},{9,1},... | collective-permute-start | bytes 393224 | tf_op jit(solution)/shard_map/ppermute | solution.py:53
  52.2 50.1 %collective-permute-start.28 = (f32[256,4096]{1,0:T(8,128)S(1)}, f32[256,4096]{1,0:T(8,128)S(1)}, u32[]{:S(2)}, u32[]{:S(2)}) collective-permute-start(f32[256,4096]{1,0:T(8,128)S(1)} %shard_map.88), channel_id=1, source_target_pairs={{0,1},{1,0},{2,3},{3,2},{4,5},{5,4},{6,7},{7,6},{8,9},{9,8},{10,11... | collective-permute-start | bytes 12582920 | tf_op jit(solution)/shard_map/ppermute | solution.py:53
  52.5 50.9 %collective-permute-start.24 = (f32[4096,256]{1,0:T(8,128)S(1)}, f32[4096,256]{1,0:T(8,128)S(1)}, u32[]{:S(2)}, u32[]{:S(2)}) collective-permute-start(f32[4096,256]{1,0:T(8,128)S(1)} %shard_map.85), channel_id=1, source_target_pairs={{0,1},{1,0},{2,3},{3,2},{4,5},{5,4},{6,7},{7,6},{8,9},{9,8},{10,11... | collective-permute-start | bytes 12582920 | tf_op jit(solution)/shard_map/ppermute | solution.py:53
  53.1 9.3 %collective-permute-start.17 = (f32[2,2,64,128]{3,2,1,0:T(8,128)S(1)}, f32[2,2,64,128]{3,2,1,0:T(8,128)S(1)}, u32[]{:S(2)}, u32[]{:S(2)}) collective-permute-start(f32[2,2,64,128]{3,2,1,0:T(8,128)S(1)} %get-tuple-element.68), channel_id=1, source_target_pairs={{0,16},{1,17},{2,18},{3,19},{4,20},{5,21},{6,22},{7,23},{8,24},{9,... | collective-permute-start | bytes 393224 | tf_op jit(solution)/shard_map/ppermute | solution.py:53
  62.5 5.0 %collective-permute-start.18 = (f32[2,2,64,128]{3,2,1,0:T(8,128)S(1)}, f32[2,2,64,128]{3,2,1,0:T(8,128)S(1)}, u32[]{:S(2)}, u32[]{:S(2)}) collective-permute-start(f32[2,2,64,128]{3,2,1,0:T(8,128)S(1)} %shard_map.79.refs_0_), channel_id=1, source_target_pairs={{0,8},{1,9},{2,10},{3,11},{4,12},{5,13},{6,14},{7,15},{8,0},{9,1},... | collective-permute-start | bytes 393224 | tf_op jit(solution)/shard_map/ppermute | solution.py:53
  67.5 5.0 %collective-permute-start.21 = (f32[4,64,128]{2,1,0:T(8,128)S(1)}, f32[4,64,128]{2,1,0:T(8,128)S(1)}, u32[]{:S(2)}, u32[]{:S(2)}) collective-permute-start(f32[4,64,128]{2,1,0:T(8,128)S(1)} %get-tuple-element.70.refs_0_), channel_id=1, source_target_pairs={{0,2},{1,3},{2,0},{3,1},{4,6},{5,7},{6,4},{7,5},{8,10},{9,11},{10,... | collective-permute-start | bytes 393224 | tf_op jit(solution)/shard_map/ppermute | solution.py:53
  68.9 6.4 %collective-permute-start.19 = (f32[4,64,128]{2,1,0:T(8,128)S(1)}, f32[4,64,128]{2,1,0:T(8,128)S(1)}, u32[]{:S(2)}, u32[]{:S(2)}) collective-permute-start(f32[4,64,128]{2,1,0:T(8,128)S(1)} %get-tuple-element.69.refs_0_), channel_id=1, source_target_pairs={{0,4},{1,5},{2,6},{3,7},{4,0},{5,1},{6,2},{7,3},{8,12},{9,13},{10,... | collective-permute-start | bytes 393224 | tf_op jit(solution)/shard_map/ppermute | solution.py:53
  72.6 6.7 %collective-permute-start.22 = (f32[8,64,128]{2,1,0:T(8,128)S(1)}, f32[8,64,128]{2,1,0:T(8,128)S(1)}, u32[]{:S(2)}, u32[]{:S(2)}) collective-permute-start(f32[8,64,128]{2,1,0:T(8,128)S(1)} %shard_map.82.refs_3_), channel_id=1, source_target_pairs={{0,4},{1,5},{2,6},{3,7},{4,0},{5,1},{6,2},{7,3},{8,12},{9,13},{10,... | collective-permute-start | bytes 786440 | tf_op jit(solution)/shard_map/ppermute | solution.py:53
  75.3 6.7 %collective-permute-start.20 = (f32[8,64,128]{2,1,0:T(8,128)S(1)}, f32[8,64,128]{2,1,0:T(8,128)S(1)}, u32[]{:S(2)}, u32[]{:S(2)}) collective-permute-start(f32[8,64,128]{2,1,0:T(8,128)S(1)} %shard_map.81.refs_1_), channel_id=1, source_target_pairs={{0,2},{1,3},{2,0},{3,1},{4,6},{5,7},{6,4},{7,5},{8,10},{9,11},{10,... | collective-permute-start | bytes 786440 | tf_op jit(solution)/shard_map/ppermute | solution.py:53
  76.4 20.6 %collective-permute-start.25 = (f32[4,2,64,128]{3,2,0,1:T(8,128)S(1)}, f32[4,2,64,128]{3,2,0,1:T(8,128)S(1)}, u32[]{:S(2)}, u32[]{:S(2)}) collective-permute-start(f32[4,2,64,128]{3,2,0,1:T(8,128)S(1)} %copy.7), channel_id=1, source_target_pairs={{0,4},{1,3},{2,6},{3,1},{4,0},{5,7},{6,2},{7,5},{8,12},{9,11},{10,... | collective-permute-start | bytes 786440 | tf_op jit(solution)/shard_map/ppermute | solution.py:53
  83.2 6.5 %collective-permute-start.29 = (f32[2,64,128]{2,1,0:T(8,128)S(1)}, f32[2,64,128]{2,1,0:T(8,128)S(1)}, u32[]{:S(2)}, u32[]{:S(2)}) collective-permute-start(f32[2,64,128]{2,1,0:T(8,128)S(1)} %get-tuple-element.71.refs_0_), channel_id=1, source_target_pairs={{0,16},{1,17},{2,18},{3,19},{4,20},{5,21},{6,22},{7,23},{8,24},{9,... | collective-permute-start | bytes 196616 | tf_op jit(solution)/shard_map/ppermute | solution.py:53
  89.7 5.0 %collective-permute-start.30 = (f32[2,2,64,128]{3,2,1,0:T(8,128)S(1)}, f32[2,2,64,128]{3,2,1,0:T(8,128)S(1)}, u32[]{:S(2)}, u32[]{:S(2)}) collective-permute-start(f32[2,2,64,128]{3,2,1,0:T(8,128)S(1)} %shard_map.90.refs_0_), channel_id=1, source_target_pairs={{0,8},{1,9},{2,10},{3,11},{4,12},{5,13},{6,14},{7,15},{8,0},{9,1},... | collective-permute-start | bytes 393224 | tf_op jit(solution)/shard_map/ppermute | solution.py:53
  94.7 5.0 %collective-permute-start.33 = (f32[4,64,128]{2,1,0:T(8,128)S(1)}, f32[4,64,128]{2,1,0:T(8,128)S(1)}, u32[]{:S(2)}, u32[]{:S(2)}) collective-permute-start(f32[4,64,128]{2,1,0:T(8,128)S(1)} %get-tuple-element.79.refs_0_), channel_id=1, source_target_pairs={{0,2},{1,3},{2,0},{3,1},{4,6},{5,7},{6,4},{7,5},{8,10},{9,11},{10,... | collective-permute-start | bytes 393224 | tf_op jit(solution)/shard_map/ppermute | solution.py:53
  95.9 5.0 %collective-permute-start.31 = (f32[4,64,128]{2,1,0:T(8,128)S(1)}, f32[4,64,128]{2,1,0:T(8,128)S(1)}, u32[]{:S(2)}, u32[]{:S(2)}) collective-permute-start(f32[4,64,128]{2,1,0:T(8,128)S(1)} %get-tuple-element.78.refs_0_), channel_id=1, source_target_pairs={{0,4},{1,5},{2,6},{3,7},{4,0},{5,1},{6,2},{7,3},{8,12},{9,13},{10,... | collective-permute-start | bytes 393224 | tf_op jit(solution)/shard_map/ppermute | solution.py:53
  97.1 5.1 %collective-permute-start.26 = (f32[2,2,64,128]{3,2,0,1:T(8,128)S(1)}, f32[2,2,64,128]{3,2,0,1:T(8,128)S(1)}, u32[]{:S(2)}, u32[]{:S(2)}) collective-permute-start(f32[2,2,64,128]{3,2,0,1:T(8,128)S(1)} %slice.51), channel_id=1, source_target_pairs={{0,8},{1,9},{2,10},{3,11},{4,12},{5,13},{6,14},{7,15},{8,0},{9,1},... | collective-permute-start | bytes 393224 | tf_op jit(solution)/shard_map/ppermute | solution.py:53
  99.8 6.4 %collective-permute-start.34 = (f32[8,64,128]{2,1,0:T(8,128)S(1)}, f32[8,64,128]{2,1,0:T(8,128)S(1)}, u32[]{:S(2)}, u32[]{:S(2)}) collective-permute-start(f32[8,64,128]{2,1,0:T(8,128)S(1)} %shard_map.93.refs_3_), channel_id=1, source_target_pairs={{0,4},{1,5},{2,6},{3,7},{4,0},{5,1},{6,2},{7,3},{8,12},{9,13},{10,... | collective-permute-start | bytes 786440 | tf_op jit(solution)/shard_map/ppermute | solution.py:53
  100.9 6.4 %collective-permute-start.32 = (f32[8,64,128]{2,1,0:T(8,128)S(1)}, f32[8,64,128]{2,1,0:T(8,128)S(1)}, u32[]{:S(2)}, u32[]{:S(2)}) collective-permute-start(f32[8,64,128]{2,1,0:T(8,128)S(1)} %shard_map.92.refs_1_), channel_id=1, source_target_pairs={{0,2},{1,3},{2,0},{3,1},{4,6},{5,7},{6,4},{7,5},{8,10},{9,11},{10,... | collective-permute-start | bytes 786440 | tf_op jit(solution)/shard_map/ppermute | solution.py:53
  102.2 6.9 %collective-permute-start.27 = (f32[2,64,128]{2,1,0:T(8,128)S(1)}, f32[2,64,128]{2,1,0:T(8,128)S(1)}, u32[]{:S(2)}, u32[]{:S(2)}) collective-permute-start(f32[2,64,128]{2,1,0:T(8,128)S(1)} %get-tuple-element.92), channel_id=1, source_target_pairs={{0,1},{1,0},{2,3},{3,2},{4,5},{5,4},{6,7},{7,6},{8,9},{9,8},{10,11... | collective-permute-start | bytes 196616 | tf_op jit(solution)/shard_map/ppermute | solution.py:53
  110.6 6.7 %collective-permute-start.37 = (f32[8,64,128]{2,1,0:T(8,128)S(1)}, f32[8,64,128]{2,1,0:T(8,128)S(1)}, u32[]{:S(2)}, u32[]{:S(2)}) collective-permute-start(f32[8,64,128]{2,1,0:T(8,128)S(1)} %get-tuple-element.84), channel_id=1, source_target_pairs={{0,4},{1,5},{2,6},{3,7},{4,0},{5,1},{6,2},{7,3},{8,12},{9,13},{10,... | collective-permute-start | bytes 786440 | tf_op jit(solution)/shard_map/ppermute | solution.py:53
  111.8 7.0 %collective-permute-start.35 = (f32[8,64,128]{2,1,0:T(8,128)S(1)}, f32[8,64,128]{2,1,0:T(8,128)S(1)}, u32[]{:S(2)}, u32[]{:S(2)}) collective-permute-start(f32[8,64,128]{2,1,0:T(8,128)S(1)} %get-tuple-element.81), channel_id=1, source_target_pairs={{0,2},{1,3},{2,0},{3,1},{4,6},{5,7},{6,4},{7,5},{8,10},{9,11},{10,... | collective-permute-start | bytes 786440 | tf_op jit(solution)/shard_map/ppermute | solution.py:53
  117.3 5.0 %collective-permute-start.38 = (f32[4,64,128]{2,1,0:T(8,128)S(1)}, f32[4,64,128]{2,1,0:T(8,128)S(1)}, u32[]{:S(2)}, u32[]{:S(2)}) collective-permute-start(f32[4,64,128]{2,1,0:T(8,128)S(1)} %shard_map.97), channel_id=1, source_target_pairs={{0,2},{1,3},{2,0},{3,1},{4,6},{5,7},{6,4},{7,5},{8,10},{9,11},{10,... | collective-permute-start | bytes 393224 | tf_op jit(solution)/shard_map/ppermute | solution.py:53
  118.8 5.0 %collective-permute-start.36 = (f32[4,64,128]{2,1,0:T(8,128)S(1)}, f32[4,64,128]{2,1,0:T(8,128)S(1)}, u32[]{:S(2)}, u32[]{:S(2)}) collective-permute-start(f32[4,64,128]{2,1,0:T(8,128)S(1)} %shard_map.96), channel_id=1, source_target_pairs={{0,4},{1,5},{2,6},{3,7},{4,0},{5,1},{6,2},{7,3},{8,12},{9,13},{10,... | collective-permute-start | bytes 393224 | tf_op jit(solution)/shard_map/ppermute | solution.py:53
  123.9 6.4 %collective-permute-start.39 = (f32[4,2,64,128]{3,2,1,0:T(8,128)S(1)}, f32[4,2,64,128]{3,2,1,0:T(8,128)S(1)}, u32[]{:S(2)}, u32[]{:S(2)}) collective-permute-start(f32[4,2,64,128]{3,2,1,0:T(8,128)S(1)} %get-tuple-element.87), channel_id=1, source_target_pairs={{0,8},{1,9},{2,10},{3,11},{4,12},{5,13},{6,14},{7,15},{8,0},{9,1},... | collective-permute-start | bytes 786440 | tf_op jit(solution)/shard_map/ppermute | solution.py:53
  130.4 6.5 %collective-permute-start.42 = (f32[4,64,128]{2,1,0:T(8,128)S(1)}, f32[4,64,128]{2,1,0:T(8,128)S(1)}, u32[]{:S(2)}, u32[]{:S(2)}) collective-permute-start(f32[4,64,128]{2,1,0:T(8,128)S(1)} %get-tuple-element.89.refs_0_), channel_id=1, source_target_pairs={{0,2},{1,3},{2,0},{3,1},{4,6},{5,7},{6,4},{7,5},{8,10},{9,11},{10,... | collective-permute-start | bytes 393224 | tf_op jit(solution)/shard_map/ppermute | solution.py:53
  132.1 5.8 %collective-permute-start.40 = (f32[4,64,128]{2,1,0:T(8,128)S(1)}, f32[4,64,128]{2,1,0:T(8,128)S(1)}, u32[]{:S(2)}, u32[]{:S(2)}) collective-permute-start(f32[4,64,128]{2,1,0:T(8,128)S(1)} %get-tuple-element.88.refs_0_), channel_id=1, source_target_pairs={{0,4},{1,5},{2,6},{3,7},{4,0},{5,1},{6,2},{7,3},{8,12},{9,13},{10,... | collective-permute-start | bytes 393224 | tf_op jit(solution)/shard_map/ppermute | solution.py:53
  136.8 6.4 %collective-permute-start.43 = (f32[8,64,128]{2,1,0:T(8,128)S(1)}, f32[8,64,128]{2,1,0:T(8,128)S(1)}, u32[]{:S(2)}, u32[]{:S(2)}) collective-permute-start(f32[8,64,128]{2,1,0:T(8,128)S(1)} %shard_map.101.refs_3_), channel_id=1, source_target_pairs={{0,4},{1,5},{2,6},{3,7},{4,0},{5,1},{6,2},{7,3},{8,12},{9,13},{10,... | collective-permute-start | bytes 786440 | tf_op jit(solution)/shard_map/ppermute | solution.py:53
  137.9 6.4 %collective-permute-start.41 = (f32[8,64,128]{2,1,0:T(8,128)S(1)}, f32[8,64,128]{2,1,0:T(8,128)S(1)}, u32[]{:S(2)}, u32[]{:S(2)}) collective-permute-start(f32[8,64,128]{2,1,0:T(8,128)S(1)} %shard_map.100.refs_1_), channel_id=1, source_target_pairs={{0,2},{1,3},{2,0},{3,1},{4,6},{5,7},{6,4},{7,5},{8,10},{9,11},{10,... | collective-permute-start | bytes 786440 | tf_op jit(solution)/shard_map/ppermute | solution.py:53
  146.1 2.2 %collective-permute-start.44 = (f32[2,64,128]{2,1,0:T(8,128)S(1)}, f32[2,64,128]{2,1,0:T(8,128)S(1)}, u32[]{:S(2)}, u32[]{:S(2)}) collective-permute-start(f32[2,64,128]{2,1,0:T(8,128)S(1)} %get-tuple-element.91), channel_id=1, source_target_pairs={{0,1},{1,0},{2,3},{3,2},{4,5},{5,4},{6,7},{7,6},{8,9},{9,8},{10,11... | collective-permute-start | bytes 196616 | tf_op jit(solution)/shard_map/ppermute | solution.py:53
  146.2 1.4 collective-permute-start.23
  (4 other events, 14.2 us)
where the time goes:
time: 149 us
  waiting for transfers between devices  72.6 us (49%)
  starting transfers between devices  54.3 us (36%)
  Pallas kernels  17.9 us (12%)
  local copies, waits for them, and re-layouts  3.11 us (2%)
    ppermute x45, waiting for transfers between devices, permute(): return lax.ppermute(value, AXES, [(i, partner(i)) for i in range(32)])  72.6 us
    ppermute x45, starting transfers between devices, permute(): return lax.ppermute(value, AXES, [(i, partner(i)) for i in range(32)])  54.3 us
    pallas_call x34, Pallas kernels, kernel_call(): pl.pallas_call(ordered, out_shape=shapes, in_specs=[vmem] * len(ins) + [p...  15 us
    unnamed x14, local copies, waits for them, and re-layouts  3.06 us
  transfers between devices with their start and end apart: 45, of which 32 were waited for; matrix products, arithmetic and copies ran while one was open for 0% of the time, Pallas kernels for 8%

commit v1 on v0

--- a/solution.py
+++ b/solution.py
@@ -46,7 +46,8 @@
 
 
 WIDE = 64
-CORE, XBIT, YBIT, NEAR, FAR = 1, 2, 4, 8, 16
+CORE, XBIT, YBIT, ZBIT = 1, 2, 4, 8
+FAR_FIRST = (2, 3, 1)
 
 
 def permute(value, partner):
@@ -77,9 +78,6 @@
 
 def z_flip(z, k):
     return flip(z // 2, k // 2) * 2 + flip(z % 2, k % 2)
-
-
-Z_ORDER = (0, 2, 1, 3)
 
 
 def plane_at(y, x, colour, first, second):
@@ -97,7 +95,7 @@
             plane = plane_at(y, x, colour, first, second)
             for j in range(4):
                 if deep:
-                    start = ((z_flip(z, Z_ORDER[j]) * 4 + plane) * 2 + core) * 128
+                    start = ((z_flip(z, j) * 4 + plane) * 2 + core) * 128
                 else:
                     start = ((flip(z % 2, j // 2) * 4 + plane) * 2 + core) * 256 + j % 2 * 128
                 starts.append(pl.multiple_of(start, 128))
@@ -181,7 +179,7 @@
         for second in range(2):
             plane = plane_at(y, x, core, rel // 2, second)
             for j in range(4):
-                col = pl.multiple_of((z_flip(z, Z_ORDER[j]) * 8 + plane * 2 + core) * 128, 128)
+                col = pl.multiple_of((z_flip(z, j) * 8 + plane * 2 + core) * 128, 128)
                 here = (second * 4 + j) * 128
                 tops[rel][:, here : here + 128] = border_ref[:, pl.ds(col, 128)].astype(F32)
         tops[rel][:, 1024:] = sol
@@ -254,13 +252,15 @@
     return kernel_call(widen_kernel, [(w.shape, F32)], [w], after=after)[0]
 
 
-def widen_half(w, half):
-    rows = w.shape[0] // 2
-
-    def kernel(w_ref, out_ref):
-        out_ref[...] = w_ref[half * rows : (half + 1) * rows, :].astype(F32)
-
-    return kernel_call(kernel, [((rows, w.shape[1]), F32)], [w])[0]
+def widen_halves_kernel(w_ref, low_ref, high_ref):
+    rows = low_ref.shape[0]
+    low_ref[...] = w_ref[:rows, :].astype(F32)
+    high_ref[...] = w_ref[rows:, :].astype(F32)
+
+
+def widen_halves(w):
+    shape = (w.shape[0] // 2, w.shape[1])
+    return kernel_call(widen_halves_kernel, [(shape, F32)] * 2, [w])
 
 
 def join_halves(keep, recv):
@@ -406,12 +406,24 @@
     )
 
 
-def depth_load(value, deep):
-    half = value.shape[0] // 2
-    value = value[:half] + swap(value[half:], NEAR)
-    if deep:
-        value = value[:1] + swap(value[1:], FAR)
-    return value
+def along_line(parts):
+    got = {j: swap(parts[j], j * ZBIT) for j in FAR_FIRST}
+    return [got[j] for j in (1, 2, 3)]
+
+
+def cut(v):
+    return tuple(v[j] for j in range(4))
+
+
+def depth_load(keep, got):
+    parts = glue(lambda a, b: cut(a + b), keep, got)
+    (own,) = glue(lambda *p: (p[0] + p[1] + p[2] + p[3],), parts[0], *along_line(parts))
+    return own
+
+
+def pair_load(keep, got):
+    v = keep + got
+    return v[:2] + swap(v[2:], ZBIT)
 
 
 def by_core(own):
@@ -434,39 +446,28 @@
     return jnp.stack([k0 + f0[:4] + s0, k1 + f1[:4] + s1], 1)
 
 
-def depth_total(pieces, deep):
-    if not deep:
-
-        def both(*p):
-            v = colours(*p)
-            return v, jnp.concatenate([v[2:], v[:2]], 0)
-
-        value, turned = glue(both, *pieces)
-        got = swap(turned, NEAR)
-        return glue(lambda v, g: ((v + g)[:, 0], (v + g)[:, 1]), value, got), [got]
-
-    def halves(*p):
+def depth_sum(pieces):
+    parts = glue(lambda *p: cut(colours(*p)), *pieces)
+    got = along_line(parts)
+    (own,) = glue(lambda *p: (p[0] + p[1] + p[2] + p[3],), parts[0], *got)
+    return own, got
+
+
+def depth_spread(own, after=()):
+    def lines(*p):
+        return tuple(jnp.stack([v[k] for v in p]) for k in range(2))
+
+    return glue(lines, own, *along_line([own] * 4), after=after)
+
+
+def pair_total(pieces):
+    def both(*p):
         v = colours(*p)
-        return v[:2], v[2:]
-
-    keep, send = glue(halves, *pieces)
-
-    def turn(k, g):
-        v = k + g
-        return v, jnp.concatenate([v[1:], v[:1]], 0)
-
-    near = swap(send, NEAR)
-    keep, turned = glue(turn, keep, near)
-    far = swap(turned, FAR)
-    (pair,) = glue(lambda k, g: (k + g,), keep, far)
-    return lines(pair), [near, far]
-
-
-def lines(pair, after=()):
-    def put(p, g):
-        return tuple(jnp.concatenate([p[:, k], g[:, k]], 0) for k in range(2))
-
-    return glue(put, pair, swap(pair, NEAR), after=after)
+        return v, jnp.concatenate([v[2:], v[:2]], 0)
+
+    value, turned = glue(both, *pieces)
+    got = swap(turned, ZBIT)
+    return glue(lambda v, g: ((v + g)[:, 0], (v + g)[:, 1]), value, got)
 
 
 def plane_spread(pair_of_lines):
@@ -499,7 +500,6 @@
         prep_top, [((32, 1152), F32)] * 4, [border[0], solution[0]]
     )
     tops = plane_inputs(ready)
-    top_w, top_t = join_halves(winv_top, [swap(widen_half(winv_top, i), CORE) for i in range(2)])
     keep, send, sol_all = kernel_call(
         top_load_kernel,
         [((4, 2, WIDE, 128), F32)] * 2 + [((128, 128), BF16)],
@@ -507,18 +507,20 @@
         [pltpu.VMEM((128, 1024), BF16)],
         flops=2 * 128 * 1024 * 128,
     )
-    got = swap_loads(send)
-    load = by_core(depth_load(keep + got, True))
-
+    top_w, top_t = join_halves(
+        winv_top, [swap(part, CORE) for part in widen_halves(winv_top)]
+    )
+    load = by_core(depth_load(keep, swap_loads(send))[None])
+
+    parts = run_forward(top_w, load, True)
+    inner, marks = depth_sum(plane_sum(parts))
     mids = plane_inputs(
-        kernel_call(prep_mid, [((32, 1024), F32)] * 4, [border[0]], after=[got])
-    )
-
-    parts = run_forward(top_w, load, True, after=mids)
-    line, marks = depth_total(plane_sum(parts), True)
-    cou_w = join_rows(coupling, swap(widen(coupling, after=marks[:1]), CORE))
-    mid_w, mid_t = join_cols(winv_mid, swap(widen(winv_mid, after=marks[:1]), CORE))
-    pieces = plane_spread(line)
+        kernel_call(prep_mid, [((32, 1024), F32)] * 4, [border[0]], after=marks[:1])
+    )
+    pair = depth_spread(inner, after=mids)
+    cou_w = join_rows(coupling, swap(widen(coupling, after=pair[:1]), CORE))
+    mid_w, mid_t = join_cols(winv_mid, swap(widen(winv_mid, after=pair[:1]), CORE))
+    pieces = plane_spread(pair)
     adjoint, theirs = run_backward(top_t, pieces, True, True)
     top_out = unpack(adjoint, swap(theirs, CORE))
 
@@ -529,13 +531,13 @@
         [pltpu.VMEM((128, 1024), BF16)],
         flops=2 * 128 * 1024 * 128,
     )
-    load = by_core(depth_load(keep + swap_loads(send), False))
-
-    (pair,) = glue(lambda a, b: (jnp.stack([a, b]),), adjoint, swap(adjoint, FAR))
-    pieces = plane_spread(lines(pair))
-    (part,) = run_backward(cou_w, pieces, True, False)
+    got = swap_loads(send)
+    load = by_core(pair_load(keep, got))
+
+    pieces = plane_spread(depth_spread(adjoint, after=[got]))
+    (part,) = run_backward(cou_w, pieces, True, False, after=[top_out])
     parts = run_forward(mid_w, [*load, part], False)
-    pieces = plane_spread(depth_total(plane_sum(parts), False)[0])
+    pieces = plane_spread(pair_total(plane_sum(parts)))
     adjoint, theirs = run_backward(mid_t, pieces, False, True)
     return top_out, unpack(adjoint, swap(theirs, CORE))
 

time: 149 us -> 152 us (1.020)
  waiting for transfers between devices: 72.6 us -> 79 us
  starting transfers between devices: 54.3 us -> 51.1 us
  Pallas kernels: 17.9 us -> 15.9 us
    ppermute x45 -> x50, waiting for transfers between devices: 72.6 us -> 79 us  [permute(): return lax.ppermute(value, AXES, [(i, partner(i)) for i in range(32)])]
    ppermute x45 -> x50, starting transfers between devices: 54.3 us -> 51.1 us  [permute(): return lax.ppermute(value, AXES, [(i, partner(i)) for i in range(32)])]
    pallas_call x34 -> x33, Pallas kernels: 15 us -> 12.9 us  [kernel_call(): pl.pallas_call(ordered, out_shape=shapes, in_specs=[vmem] * len(ins) + [p...]
    unnamed x14 -> x16, local copies, waits for them, and re-layouts: 3.06 us -> 4.33 us
  transfers between devices with their start and end apart: 45 -> 50, of which waited for: 32 -> 33; matrix products, arithmetic and copies ran while one was open for 0% -> 0% of each run, Pallas kernels for 8% -> 6%
where the time goes in v1:
time: 152 us; the launch traced here: 151 us
  waiting for transfers between devices  79 us (52%)
  starting transfers between devices  51.1 us (34%)
  Pallas kernels  15.9 us (10%)
  local copies, waits for them, and re-layouts  4.38 us (3%)
    ppermute x50, waiting for transfers between devices, permute(): return lax.ppermute(value, AXES, [(i, partner(i)) for i in range(32)])  79 us
    ppermute x50, starting transfers between devices, permute(): return lax.ppermute(value, AXES, [(i, partner(i)) for i in range(32)])  51.1 us
    pallas_call x33, Pallas kernels, kernel_call(): pl.pallas_call(ordered, out_shape=shapes, in_specs=[vmem] * len(ins) + [p...  12.9 us
    unnamed x16, local copies, waits for them, and re-layouts  4.33 us
  transfers between devices with their start and end apart: 50, of which 33 were waited for; matrix products, arithmetic and copies ran while one was open for 0% of the time, Pallas kernels for 6%

profile of v1, /device:TPU:0, one launch (start us, length us, event | category | flops | bytes accessed | tf_op | source)
XLA Modules:
  0.0 151.4 jit_solution(13983428909286541600)
XLA Ops:
  0.6 1.2 copy-done.2
  1.9 1.4 shard_map.68
  6.1 2.6 %collective-permute-start.3 = (f32[32,1152]{1,0:T(8,128)S(1)}, f32[32,1152]{1,0:T(8,128)S(1)}, u32[]{:S(2)}, u32[]{:S(2)}) collective-permute-start(f32[32,1152]{1,0:T(8,128)S(1)} %get-tuple-element.59), channel_id=1, source_target_pairs={{0,2},{1,5},{2,0},{3,7},{4,6},{5,1},{6,4},{7,3},{8,10},{9,13},{10,... | collective-permute-start | bytes 442376 | tf_op jit(solution)/shard_map/ppermute | solution.py:54
  8.8 3.6 %collective-permute-done.3.refs_2_ = f32[32,1152]{1,0:T(8,128)S(1)} collective-permute-done((f32[32,1152]{1,0:T(8,128)S(1)}, f32[32,1152]{1,0:T(8,128)S(1)}, u32[]{:S(2)}, u32[]{:S(2)}) %collective-permute-start.3) | collective-permute-done | bytes 147488 | tf_op jit(solution)/shard_map/ppermute | solution.py:54
  13.9 2.1 %collective-permute-start.5 = (f32[4,2,64,128]{3,2,1,0:T(8,128)S(1)}, f32[4,2,64,128]{3,2,1,0:T(8,128)S(1)}, u32[]{:S(2)}, u32[]{:S(2)}) collective-permute-start(f32[4,2,64,128]{3,2,1,0:T(8,128)S(1)} %get-tuple-element.62), channel_id=1, source_target_pairs={{0,4},{1,3},{2,6},{3,1},{4,0},{5,7},{6,2},{7,5},{8,12},{9,11},{10,... | collective-permute-start | bytes 786440 | tf_op jit(solution)/shard_map/ppermute | solution.py:54
  16.1 4.4 %collective-permute-done.5.refs_1_ = f32[4,2,64,128]{3,2,1,0:T(8,128)S(1)} collective-permute-done((f32[4,2,64,128]{3,2,1,0:T(8,128)S(1)}, f32[4,2,64,128]{3,2,1,0:T(8,128)S(1)}, u32[]{:S(2)}, u32[]{:S(2)}) %collective-permute-start.5) | collective-permute-done | bytes 262176 | tf_op jit(solution)/shard_map/ppermute | solution.py:54
  20.5 2.1 %collective-permute-start.6 = (f32[2,64,128]{2,1,0:T(8,128)S(1)}, f32[2,64,128]{2,1,0:T(8,128)S(1)}, u32[]{:S(2)}, u32[]{:S(2)}) collective-permute-start(f32[2,64,128]{2,1,0:T(8,128)S(1)} %get-tuple-element.64), channel_id=1, source_target_pairs={{0,8},{1,9},{2,10},{3,11},{4,12},{5,13},{6,14},{7,15},{8,0},{9,1},... | collective-permute-start | bytes 196616 | tf_op jit(solution)/shard_map/ppermute | solution.py:54
  22.6 2.6 %collective-permute-start.7 = (f32[2,64,128]{2,1,0:T(8,128)S(1)}, f32[2,64,128]{2,1,0:T(8,128)S(1)}, u32[]{:S(2)}, u32[]{:S(2)}) collective-permute-start(f32[2,64,128]{2,1,0:T(8,128)S(1)} %get-tuple-element.65), channel_id=1, source_target_pairs={{0,16},{1,17},{2,18},{3,19},{4,20},{5,21},{6,22},{7,23},{8,24},{9,... | collective-permute-start | bytes 196616 | tf_op jit(solution)/shard_map/ppermute | solution.py:54
  25.2 4.0 %collective-permute-done.7.refs_2_ = f32[2,64,128]{2,1,0:T(8,128)S(1)} collective-permute-done((f32[2,64,128]{2,1,0:T(8,128)S(1)}, f32[2,64,128]{2,1,0:T(8,128)S(1)}, u32[]{:S(2)}, u32[]{:S(2)}) %collective-permute-start.7) | collective-permute-done | bytes 65568 | tf_op jit(solution)/shard_map/ppermute | solution.py:54
  29.2 2.1 %collective-permute-done.8.refs_3_ = f32[2,64,128]{2,1,0:T(8,128)S(1)} collective-permute-done((f32[2,64,128]{2,1,0:T(8,128)S(1)}, f32[2,64,128]{2,1,0:T(8,128)S(1)}, u32[]{:S(2)}, u32[]{:S(2)}) %collective-permute-start.8) | collective-permute-done | bytes 65568 | tf_op jit(solution)/shard_map/ppermute | solution.py:54
  31.4 1.3 copy-done.3
  34.5 1.6 %collective-permute-start.12 = (f32[8,64,128]{2,1,0:T(8,128)S(1)}, f32[8,64,128]{2,1,0:T(8,128)S(1)}, u32[]{:S(2)}, u32[]{:S(2)}) collective-permute-start(f32[8,64,128]{2,1,0:T(8,128)S(1)} %get-tuple-element.71), channel_id=1, source_target_pairs={{0,4},{1,5},{2,6},{3,7},{4,0},{5,1},{6,2},{7,3},{8,12},{9,13},{10,... | collective-permute-start | bytes 786440 | tf_op jit(solution)/shard_map/ppermute | solution.py:54
  36.1 1.5 collective-permute-start.10
  37.5 5.6 %collective-permute-done.12.refs_1_.refs_4_ = f32[8,64,128]{2,1,0:T(8,128)S(1)} collective-permute-done((f32[8,64,128]{2,1,0:T(8,128)S(1)}, f32[8,64,128]{2,1,0:T(8,128)S(1)}, u32[]{:S(2)}, u32[]{:S(2)}) %collective-permute-start.12) | collective-permute-done | bytes 262176 | tf_op jit(solution)/shard_map/ppermute | solution.py:54
  43.1 1.5 %collective-permute-start.13 = (f32[4,64,128]{2,1,0:T(8,128)S(1)}, f32[4,64,128]{2,1,0:T(8,128)S(1)}, u32[]{:S(2)}, u32[]{:S(2)}) collective-permute-start(f32[4,64,128]{2,1,0:T(8,128)S(1)} %shard_map.76), channel_id=1, source_target_pairs={{0,2},{1,3},{2,0},{3,1},{4,6},{5,7},{6,4},{7,5},{8,10},{9,11},{10,... | collective-permute-start | bytes 393224 | tf_op jit(solution)/shard_map/ppermute | solution.py:54
  44.7 1.6 %collective-permute-start.11 = (f32[4,64,128]{2,1,0:T(8,128)S(1)}, f32[4,64,128]{2,1,0:T(8,128)S(1)}, u32[]{:S(2)}, u32[]{:S(2)}) collective-permute-start(f32[4,64,128]{2,1,0:T(8,128)S(1)} %shard_map.75), channel_id=1, source_target_pairs={{0,4},{1,5},{2,6},{3,7},{4,0},{5,1},{6,2},{7,3},{8,12},{9,13},{10,... | collective-permute-start | bytes 393224 | tf_op jit(solution)/shard_map/ppermute | solution.py:54
  46.3 1.9 %collective-permute-done.13.refs_5_ = f32[4,64,128]{2,1,0:T(8,128)S(1)} collective-permute-done((f32[4,64,128]{2,1,0:T(8,128)S(1)}, f32[4,64,128]{2,1,0:T(8,128)S(1)}, u32[]{:S(2)}, u32[]{:S(2)}) %collective-permute-start.13) | collective-permute-done | bytes 131104 | tf_op jit(solution)/shard_map/ppermute | solution.py:54
  48.2 1.5 %collective-permute-done.11.refs_2_ = f32[4,64,128]{2,1,0:T(8,128)S(1)} collective-permute-done((f32[4,64,128]{2,1,0:T(8,128)S(1)}, f32[4,64,128]{2,1,0:T(8,128)S(1)}, u32[]{:S(2)}, u32[]{:S(2)}) %collective-permute-start.11) | collective-permute-done | bytes 131104 | tf_op jit(solution)/shard_map/ppermute | solution.py:54
  49.9 1.5 collective-permute-start.15
  51.4 2.9 %collective-permute-start.16 = (f32[2,64,128]{2,1,0:T(8,128)S(1)}, f32[2,64,128]{2,1,0:T(8,128)S(1)}, u32[]{:S(2)}, u32[]{:S(2)}) collective-permute-start(f32[2,64,128]{2,1,0:T(8,128)S(1)} %get-tuple-element.76), channel_id=1, source_target_pairs={{0,24},{1,25},{2,26},{3,27},{4,28},{5,29},{6,30},{7,31},{8,16},{9,... | collective-permute-start | bytes 196616 | tf_op jit(solution)/shard_map/ppermute | solution.py:54
  55.5 2.0 %collective-permute-done.16.refs_3_ = f32[2,64,128]{2,1,0:T(8,128)S(1)} collective-permute-done((f32[2,64,128]{2,1,0:T(8,128)S(1)}, f32[2,64,128]{2,1,0:T(8,128)S(1)}, u32[]{:S(2)}, u32[]{:S(2)}) %collective-permute-start.16) | collective-permute-done | bytes 65568 | tf_op jit(solution)/shard_map/ppermute | solution.py:54
  59.5 2.6 %collective-permute-start.18 = (f32[2,64,128]{2,1,0:T(8,128)S(1)}, f32[2,64,128]{2,1,0:T(8,128)S(1)}, u32[]{:S(2)}, u32[]{:S(2)}) collective-permute-start(f32[2,64,128]{2,1,0:T(8,128)S(1)} %shard_map.78.refs_0_), channel_id=1, source_target_pairs={{0,16},{1,17},{2,18},{3,19},{4,20},{5,21},{6,22},{7,23},{8,24},{9,... | collective-permute-start | bytes 196616 | tf_op jit(solution)/shard_map/ppermute | solution.py:54
  62.1 2.7 %collective-permute-start.19 = (f32[2,64,128]{2,1,0:T(8,128)S(1)}, f32[2,64,128]{2,1,0:T(8,128)S(1)}, u32[]{:S(2)}, u32[]{:S(2)}) collective-permute-start(f32[2,64,128]{2,1,0:T(8,128)S(1)} %shard_map.78.refs_0_), channel_id=1, source_target_pairs={{0,24},{1,25},{2,26},{3,27},{4,28},{5,29},{6,30},{7,31},{8,16},{9,... | collective-permute-start | bytes 196616 | tf_op jit(solution)/shard_map/ppermute | solution.py:54
  64.8 1.9 %collective-permute-done.18.refs_2_ = f32[2,64,128]{2,1,0:T(8,128)S(1)} collective-permute-done((f32[2,64,128]{2,1,0:T(8,128)S(1)}, f32[2,64,128]{2,1,0:T(8,128)S(1)}, u32[]{:S(2)}, u32[]{:S(2)}) %collective-permute-start.18) | collective-permute-done | bytes 65568 | tf_op jit(solution)/shard_map/ppermute | solution.py:54
  66.7 2.1 %collective-permute-done.19.refs_3_ = f32[2,64,128]{2,1,0:T(8,128)S(1)} collective-permute-done((f32[2,64,128]{2,1,0:T(8,128)S(1)}, f32[2,64,128]{2,1,0:T(8,128)S(1)}, u32[]{:S(2)}, u32[]{:S(2)}) %collective-permute-start.19) | collective-permute-done | bytes 65568 | tf_op jit(solution)/shard_map/ppermute | solution.py:54
  72.3 3.2 %collective-permute-done.25.refs_1_ = f32[4,64,128]{2,1,0:T(8,128)S(1)} collective-permute-done((f32[4,64,128]{2,1,0:T(8,128)S(1)}, f32[4,64,128]{2,1,0:T(8,128)S(1)}, u32[]{:S(2)}, u32[]{:S(2)}) %collective-permute-start.25) | collective-permute-done | bytes 131104 | tf_op jit(solution)/shard_map/ppermute | solution.py:54
  76.8 1.2 collective-permute-start.24
  79.5 3.6 %collective-permute-done.26.refs_4_ = f32[8,64,128]{2,1,0:T(8,128)S(1)} collective-permute-done((f32[8,64,128]{2,1,0:T(8,128)S(1)}, f32[8,64,128]{2,1,0:T(8,128)S(1)}, u32[]{:S(2)}, u32[]{:S(2)}) %collective-permute-start.26) | collective-permute-done | bytes 262176 | tf_op jit(solution)/shard_map/ppermute | solution.py:54
  83.1 3.0 %collective-permute-done.24.refs_2_ = f32[8,64,128]{2,1,0:T(8,128)S(1)} collective-permute-done((f32[8,64,128]{2,1,0:T(8,128)S(1)}, f32[8,64,128]{2,1,0:T(8,128)S(1)}, u32[]{:S(2)}, u32[]{:S(2)}) %collective-permute-start.24) | collective-permute-done | bytes 262176 | tf_op jit(solution)/shard_map/ppermute | solution.py:54
  88.2 2.3 %collective-permute-start.34 = (f32[2,64,128]{2,1,0:T(8,128)S(1)}, f32[2,64,128]{2,1,0:T(8,128)S(1)}, u32[]{:S(2)}, u32[]{:S(2)}) collective-permute-start(f32[2,64,128]{2,1,0:T(8,128)S(1)} %get-tuple-element.83.refs_0_), channel_id=1, source_target_pairs={{0,16},{1,17},{2,18},{3,19},{4,20},{5,21},{6,22},{7,23},{8,24},{9,... | collective-permute-start | bytes 196616 | tf_op jit(solution)/shard_map/ppermute | solution.py:54
  92.3 1.8 %collective-permute-done.34.refs_2_ = f32[2,64,128]{2,1,0:T(8,128)S(1)} collective-permute-done((f32[2,64,128]{2,1,0:T(8,128)S(1)}, f32[2,64,128]{2,1,0:T(8,128)S(1)}, u32[]{:S(2)}, u32[]{:S(2)}) %collective-permute-start.34) | collective-permute-done | bytes 65568 | tf_op jit(solution)/shard_map/ppermute | solution.py:54
  94.1 2.6 %collective-permute-done.35.refs_3_ = f32[2,64,128]{2,1,0:T(8,128)S(1)} collective-permute-done((f32[2,64,128]{2,1,0:T(8,128)S(1)}, f32[2,64,128]{2,1,0:T(8,128)S(1)}, u32[]{:S(2)}, u32[]{:S(2)}) %collective-permute-start.35) | collective-permute-done | bytes 65568 | tf_op jit(solution)/shard_map/ppermute | solution.py:54
  98.5 3.3 %collective-permute-done.38.refs_1_ = f32[4,64,128]{2,1,0:T(8,128)S(1)} collective-permute-done((f32[4,64,128]{2,1,0:T(8,128)S(1)}, f32[4,64,128]{2,1,0:T(8,128)S(1)}, u32[]{:S(2)}, u32[]{:S(2)}) %collective-permute-start.38) | collective-permute-done | bytes 131104 | tf_op jit(solution)/shard_map/ppermute | solution.py:54
  106.2 1.8 %shard_map.86 = (bf16[4096,512]{1,0:T(8,128)(2,1)S(1)}, bf16[512,4096]{1,0:T(8,128)(2,1)S(1)}) custom-call(bf16[4096,256]{1,0:T(8,128)(2,1)S(1)} %copy-done.1, f32[4096,256]{1,0:T(8,128)S(1)} %collective-permute-done.28.recv_ref), custom_call_target="tpu_custom_call" | custom-call | bytes 14680064 | tf_op jit(solution)/shard_map/pallas_call | solution.py:294
  108.0 2.6 %collective-permute-done.39.refs_4_ = f32[8,64,128]{2,1,0:T(8,128)S(1)} collective-permute-done((f32[8,64,128]{2,1,0:T(8,128)S(1)}, f32[8,64,128]{2,1,0:T(8,128)S(1)}, u32[]{:S(2)}, u32[]{:S(2)}) %collective-permute-start.39) | collective-permute-done | bytes 262176 | tf_op jit(solution)/shard_map/ppermute | solution.py:54
  110.7 1.7 %shard_map.93.refs_3_ = f32[4,64,128]{2,1,0:T(8,128)S(1)} custom-call(bf16[512,4096]{1,0:T(8,128)(2,1)S(1)} %shard_map.89.refs_0_, f32[8,64,128]{2,1,0:T(8,128)S(1)} %shard_map.91.refs_1_, f32[8,64,128]{2,1,0:T(8,128)S(1)} %collective-permute-done.37.refs_2_, f32[8,64,128]{2,1,0:T(8,128)S(1)} %shard_map.92.refs_3_, ...), custom_call_target="tpu_custom_call" | custom-call | flops 536870912 | bytes 5373952 | tf_op jit(solution)/shard_map/pallas_call | solution.py:116
  112.5 1.5 %shard_map.94 = (f32[8,64,128]{2,1,0:T(8,128)S(1)}, f32[4,64,128]{2,1,0:T(8,128)S(1)}, f32[4,64,128]{2,1,0:T(8,128)S(1)}, f32[8,64,128]{2,1,0:T(8,128)S(1)}, f32...) custom-call(bf16[4096,512]{1,0:T(8,128)(2,1)S(1)} %get-tuple-element.86.refs_0_, ...), custom_call_target="tpu_custom_call" | custom-call | flops 536870912 | bytes 5505024 | tf_op jit(solution)/shard_map/pallas_call | solution.py:116
  114.0 1.8 %collective-permute-start.42 = (f32[8,64,128]{2,1,0:T(8,128)S(1)}, f32[8,64,128]{2,1,0:T(8,128)S(1)}, u32[]{:S(2)}, u32[]{:S(2)}) collective-permute-start(f32[8,64,128]{2,1,0:T(8,128)S(1)} %get-tuple-element.96), channel_id=1, source_target_pairs={{0,4},{1,5},{2,6},{3,7},{4,0},{5,1},{6,2},{7,3},{8,12},{9,13},{10,... | collective-permute-start | bytes 786440 | tf_op jit(solution)/shard_map/ppermute | solution.py:54
  116.2 5.3 %collective-permute-done.42.refs_1_.refs_4_ = f32[8,64,128]{2,1,0:T(8,128)S(1)} collective-permute-done((f32[8,64,128]{2,1,0:T(8,128)S(1)}, f32[8,64,128]{2,1,0:T(8,128)S(1)}, u32[]{:S(2)}, u32[]{:S(2)}) %collective-permute-start.42) | collective-permute-done | bytes 262176 | tf_op jit(solution)/shard_map/ppermute | solution.py:54
  123.3 3.2 %collective-permute-done.43.refs_5_ = f32[4,64,128]{2,1,0:T(8,128)S(1)} collective-permute-done((f32[4,64,128]{2,1,0:T(8,128)S(1)}, f32[4,64,128]{2,1,0:T(8,128)S(1)}, u32[]{:S(2)}, u32[]{:S(2)}) %collective-permute-start.43) | collective-permute-done | bytes 131104 | tf_op jit(solution)/shard_map/ppermute | solution.py:54
  126.6 1.4 collective-permute-done.41.refs_2_
  128.1 6.3 %collective-permute-done.44.refs_1_ = f32[4,2,64,128]{3,2,1,0:T(8,128)S(1)} collective-permute-done((f32[4,2,64,128]{3,2,1,0:T(8,128)S(1)}, f32[4,2,64,128]{3,2,1,0:T(8,128)S(1)}, u32[]{:S(2)}, u32[]{:S(2)}) %collective-permute-start.44) | collective-permute-done | bytes 262176 | tf_op jit(solution)/shard_map/ppermute | solution.py:54
  135.2 1.5 collective-permute-start.45
  136.8 4.1 %collective-permute-done.47.refs_1_ = f32[4,64,128]{2,1,0:T(8,128)S(1)} collective-permute-done((f32[4,64,128]{2,1,0:T(8,128)S(1)}, f32[4,64,128]{2,1,0:T(8,128)S(1)}, u32[]{:S(2)}, u32[]{:S(2)}) %collective-permute-start.47) | collective-permute-done | bytes 131104 | tf_op jit(solution)/shard_map/ppermute | solution.py:54
  141.0 2.2 %collective-permute-start.46 = (f32[8,64,128]{2,1,0:T(8,128)S(1)}, f32[8,64,128]{2,1,0:T(8,128)S(1)}, u32[]{:S(2)}, u32[]{:S(2)}) collective-permute-start(f32[8,64,128]{2,1,0:T(8,128)S(1)} %shard_map.99.refs_1_), channel_id=1, source_target_pairs={{0,2},{1,3},{2,0},{3,1},{4,6},{5,7},{6,4},{7,5},{8,10},{9,11},{10,... | collective-permute-start | bytes 786440 | tf_op jit(solution)/shard_map/ppermute | solution.py:54
  143.3 4.1 %collective-permute-done.48.refs_4_ = f32[8,64,128]{2,1,0:T(8,128)S(1)} collective-permute-done((f32[8,64,128]{2,1,0:T(8,128)S(1)}, f32[8,64,128]{2,1,0:T(8,128)S(1)}, u32[]{:S(2)}, u32[]{:S(2)}) %collective-permute-start.48) | collective-permute-done | bytes 262176 | tf_op jit(solution)/shard_map/ppermute | solution.py:54
  147.6 1.7 %shard_map.101 = (f32[4,64,128]{2,1,0:T(8,128)S(1)}, f32[2,64,128]{2,1,0:T(8,128)S(1)}) custom-call(bf16[512,4096]{1,0:T(8,128)(2,1)S(1)} %get-tuple-element.85.refs_0_, f32[8,64,128]{2,1,0:T(8,128)S(1)} %shard_map.99.refs_1_, f32[8,64,128]{2,1,0:T(8,128)S(1)} %collective-permute-done.46.refs_2_, f32[8,64,128]{2,1,0:T(8,128)S(1)} %shard_map.100.refs_3_, ...), custom_call_target="tpu_custom_call" | custom-call | flops 536870912 | bytes 5439488 | tf_op jit(solution)/shard_map/pallas_call | solution.py:116
  149.4 1.2 collective-permute-done.49.refs_1_
  (110 shorter events, 30.6 us)
Async XLA Ops:
  3.3 28.1 %collective-permute-start = (f32[2048,128]{1,0:T(8,128)}, f32[2048,128]{1,0:T(8,128)S(1)}, u32[]{:S(2)}, u32[]{:S(2)}) collective-permute-start(f32[2048,128]{1,0:T(8,128)} %get-tuple-element.53), channel_id=1, source_target_pairs={{0,1},{1,0},{2,3},{3,2},{4,5},{5,4},{6,7},{7,6},{8,9},{9,8},{10,11... | collective-permute-start | bytes 3145736 | tf_op jit(solution)/shard_map/ppermute | solution.py:54
  3.7 27.7 %collective-permute-start.1 = (f32[2048,128]{1,0:T(8,128)}, f32[2048,128]{1,0:T(8,128)S(1)}, u32[]{:S(2)}, u32[]{:S(2)}) collective-permute-start(f32[2048,128]{1,0:T(8,128)} %get-tuple-element.54), channel_id=1, source_target_pairs={{0,1},{1,0},{2,3},{3,2},{4,5},{5,4},{6,7},{7,6},{8,9},{9,8},{10,11... | collective-permute-start | bytes 3145736 | tf_op jit(solution)/shard_map/ppermute | solution.py:54
  5.6 3.2 %collective-permute-start.2 = (f32[32,1152]{1,0:T(8,128)S(1)}, f32[32,1152]{1,0:T(8,128)S(1)}, u32[]{:S(2)}, u32[]{:S(2)}) collective-permute-start(f32[32,1152]{1,0:T(8,128)S(1)} %get-tuple-element.58), channel_id=1, source_target_pairs={{0,1},{1,0},{2,3},{3,2},{4,5},{5,4},{6,7},{7,6},{8,9},{9,8},{10,11... | collective-permute-start | bytes 442376 | tf_op jit(solution)/shard_map/ppermute | solution.py:54
  6.1 6.3 %collective-permute-start.3 = (f32[32,1152]{1,0:T(8,128)S(1)}, f32[32,1152]{1,0:T(8,128)S(1)}, u32[]{:S(2)}, u32[]{:S(2)}) collective-permute-start(f32[32,1152]{1,0:T(8,128)S(1)} %get-tuple-element.59), channel_id=1, source_target_pairs={{0,2},{1,5},{2,0},{3,7},{4,6},{5,1},{6,4},{7,3},{8,10},{9,13},{10,... | collective-permute-start | bytes 442376 | tf_op jit(solution)/shard_map/ppermute | solution.py:54
  8.7 4.7 %collective-permute-start.4 = (f32[32,1152]{1,0:T(8,128)S(1)}, f32[32,1152]{1,0:T(8,128)S(1)}, u32[]{:S(2)}, u32[]{:S(2)}) collective-permute-start(f32[32,1152]{1,0:T(8,128)S(1)} %get-tuple-element.60), channel_id=1, source_target_pairs={{0,5},{1,2},{2,7},{3,0},{4,1},{5,6},{6,3},{7,4},{8,13},{9,10},{10,... | collective-permute-start | bytes 442376 | tf_op jit(solution)/shard_map/ppermute | solution.py:54
  13.9 6.5 %collective-permute-start.5 = (f32[4,2,64,128]{3,2,1,0:T(8,128)S(1)}, f32[4,2,64,128]{3,2,1,0:T(8,128)S(1)}, u32[]{:S(2)}, u32[]{:S(2)}) collective-permute-start(f32[4,2,64,128]{3,2,1,0:T(8,128)S(1)} %get-tuple-element.62), channel_id=1, source_target_pairs={{0,4},{1,3},{2,6},{3,1},{4,0},{5,7},{6,2},{7,5},{8,12},{9,11},{10,... | collective-permute-start | bytes 786440 | tf_op jit(solution)/shard_map/ppermute | solution.py:54
  20.5 4.7 %collective-permute-start.6 = (f32[2,64,128]{2,1,0:T(8,128)S(1)}, f32[2,64,128]{2,1,0:T(8,128)S(1)}, u32[]{:S(2)}, u32[]{:S(2)}) collective-permute-start(f32[2,64,128]{2,1,0:T(8,128)S(1)} %get-tuple-element.64), channel_id=1, source_target_pairs={{0,8},{1,9},{2,10},{3,11},{4,12},{5,13},{6,14},{7,15},{8,0},{9,1},... | collective-permute-start | bytes 196616 | tf_op jit(solution)/shard_map/ppermute | solution.py:54
  22.6 6.6 %collective-permute-start.7 = (f32[2,64,128]{2,1,0:T(8,128)S(1)}, f32[2,64,128]{2,1,0:T(8,128)S(1)}, u32[]{:S(2)}, u32[]{:S(2)}) collective-permute-start(f32[2,64,128]{2,1,0:T(8,128)S(1)} %get-tuple-element.65), channel_id=1, source_target_pairs={{0,16},{1,17},{2,18},{3,19},{4,20},{5,21},{6,22},{7,23},{8,24},{9,... | collective-permute-start | bytes 196616 | tf_op jit(solution)/shard_map/ppermute | solution.py:54
  25.2 6.1 %collective-permute-start.8 = (f32[2,64,128]{2,1,0:T(8,128)S(1)}, f32[2,64,128]{2,1,0:T(8,128)S(1)}, u32[]{:S(2)}, u32[]{:S(2)}) collective-permute-start(f32[2,64,128]{2,1,0:T(8,128)S(1)} %get-tuple-element.66), channel_id=1, source_target_pairs={{0,24},{1,25},{2,26},{3,27},{4,28},{5,29},{6,30},{7,31},{8,16},{9,... | collective-permute-start | bytes 196616 | tf_op jit(solution)/shard_map/ppermute | solution.py:54
  34.5 8.6 %collective-permute-start.12 = (f32[8,64,128]{2,1,0:T(8,128)S(1)}, f32[8,64,128]{2,1,0:T(8,128)S(1)}, u32[]{:S(2)}, u32[]{:S(2)}) collective-permute-start(f32[8,64,128]{2,1,0:T(8,128)S(1)} %get-tuple-element.71), channel_id=1, source_target_pairs={{0,4},{1,5},{2,6},{3,7},{4,0},{5,1},{6,2},{7,3},{8,12},{9,13},{10,... | collective-permute-start | bytes 786440 | tf_op jit(solution)/shard_map/ppermute | solution.py:54
  36.1 8.6 %collective-permute-start.10 = (f32[8,64,128]{2,1,0:T(8,128)S(1)}, f32[8,64,128]{2,1,0:T(8,128)S(1)}, u32[]{:S(2)}, u32[]{:S(2)}) collective-permute-start(f32[8,64,128]{2,1,0:T(8,128)S(1)} %get-tuple-element.68), channel_id=1, source_target_pairs={{0,2},{1,3},{2,0},{3,1},{4,6},{5,7},{6,4},{7,5},{8,10},{9,11},{10,... | collective-permute-start | bytes 786440 | tf_op jit(solution)/shard_map/ppermute | solution.py:54
  43.1 5.0 %collective-permute-start.13 = (f32[4,64,128]{2,1,0:T(8,128)S(1)}, f32[4,64,128]{2,1,0:T(8,128)S(1)}, u32[]{:S(2)}, u32[]{:S(2)}) collective-permute-start(f32[4,64,128]{2,1,0:T(8,128)S(1)} %shard_map.76), channel_id=1, source_target_pairs={{0,2},{1,3},{2,0},{3,1},{4,6},{5,7},{6,4},{7,5},{8,10},{9,11},{10,... | collective-permute-start | bytes 393224 | tf_op jit(solution)/shard_map/ppermute | solution.py:54
  44.7 5.0 %collective-permute-start.11 = (f32[4,64,128]{2,1,0:T(8,128)S(1)}, f32[4,64,128]{2,1,0:T(8,128)S(1)}, u32[]{:S(2)}, u32[]{:S(2)}) collective-permute-start(f32[4,64,128]{2,1,0:T(8,128)S(1)} %shard_map.75), channel_id=1, source_target_pairs={{0,4},{1,5},{2,6},{3,7},{4,0},{5,1},{6,2},{7,3},{8,12},{9,13},{10,... | collective-permute-start | bytes 393224 | tf_op jit(solution)/shard_map/ppermute | solution.py:54
  49.8 5.0 %collective-permute-start.14 = (f32[2,64,128]{2,1,0:T(8,128)S(1)}, f32[2,64,128]{2,1,0:T(8,128)S(1)}, u32[]{:S(2)}, u32[]{:S(2)}) collective-permute-start(f32[2,64,128]{2,1,0:T(8,128)S(1)} %get-tuple-element.74), channel_id=1, source_target_pairs={{0,8},{1,9},{2,10},{3,11},{4,12},{5,13},{6,14},{7,15},{8,0},{9,1},... | collective-permute-start | bytes 196616 | tf_op jit(solution)/shard_map/ppermute | solution.py:54
  49.9 5.7 %collective-permute-start.15 = (f32[2,64,128]{2,1,0:T(8,128)S(1)}, f32[2,64,128]{2,1,0:T(8,128)S(1)}, u32[]{:S(2)}, u32[]{:S(2)}) collective-permute-start(f32[2,64,128]{2,1,0:T(8,128)S(1)} %get-tuple-element.75), channel_id=1, source_target_pairs={{0,16},{1,17},{2,18},{3,19},{4,20},{5,21},{6,22},{7,23},{8,24},{9,... | collective-permute-start | bytes 196616 | tf_op jit(solution)/shard_map/ppermute | solution.py:54
  51.4 6.1 %collective-permute-start.16 = (f32[2,64,128]{2,1,0:T(8,128)S(1)}, f32[2,64,128]{2,1,0:T(8,128)S(1)}, u32[]{:S(2)}, u32[]{:S(2)}) collective-permute-start(f32[2,64,128]{2,1,0:T(8,128)S(1)} %get-tuple-element.76), channel_id=1, source_target_pairs={{0,24},{1,25},{2,26},{3,27},{4,28},{5,29},{6,30},{7,31},{8,16},{9,... | collective-permute-start | bytes 196616 | tf_op jit(solution)/shard_map/ppermute | solution.py:54
  54.9 13.9 %collective-permute-start.20 = (f32[32,1024]{1,0:T(8,128)S(1)}, f32[32,1024]{1,0:T(8,128)S(1)}, u32[]{:S(2)}, u32[]{:S(2)}) collective-permute-start(f32[32,1024]{1,0:T(8,128)S(1)} %get-tuple-element.78), channel_id=1, source_target_pairs={{0,1},{1,0},{2,3},{3,2},{4,5},{5,4},{6,7},{7,6},{8,9},{9,8},{10,11... | collective-permute-start | bytes 393224 | tf_op jit(solution)/shard_map/ppermute | solution.py:54
  57.5 4.6 %collective-permute-start.17 = (f32[2,64,128]{2,1,0:T(8,128)S(1)}, f32[2,64,128]{2,1,0:T(8,128)S(1)}, u32[]{:S(2)}, u32[]{:S(2)}) collective-permute-start(f32[2,64,128]{2,1,0:T(8,128)S(1)} %shard_map.78.refs_0_), channel_id=1, source_target_pairs={{0,8},{1,9},{2,10},{3,11},{4,12},{5,13},{6,14},{7,15},{8,0},{9,1},... | collective-permute-start | bytes 196616 | tf_op jit(solution)/shard_map/ppermute | solution.py:54
  58.4 10.5 %collective-permute-start.21 = (f32[32,1024]{1,0:T(8,128)S(1)}, f32[32,1024]{1,0:T(8,128)S(1)}, u32[]{:S(2)}, u32[]{:S(2)}) collective-permute-start(f32[32,1024]{1,0:T(8,128)S(1)} %get-tuple-element.79), channel_id=1, source_target_pairs={{0,2},{1,5},{2,0},{3,7},{4,6},{5,1},{6,4},{7,3},{8,10},{9,13},{10,... | collective-permute-start | bytes 393224 | tf_op jit(solution)/shard_map/ppermute | solution.py:54
  59.5 9.3 %collective-permute-start.22 = (f32[32,1024]{1,0:T(8,128)S(1)}, f32[32,1024]{1,0:T(8,128)S(1)}, u32[]{:S(2)}, u32[]{:S(2)}) collective-permute-start(f32[32,1024]{1,0:T(8,128)S(1)} %get-tuple-element.80), channel_id=1, source_target_pairs={{0,5},{1,2},{2,7},{3,0},{4,1},{5,6},{6,3},{7,4},{8,13},{9,10},{10,... | collective-permute-start | bytes 393224 | tf_op jit(solution)/shard_map/ppermute | solution.py:54
  59.5 7.2 %collective-permute-start.18 = (f32[2,64,128]{2,1,0:T(8,128)S(1)}, f32[2,64,128]{2,1,0:T(8,128)S(1)}, u32[]{:S(2)}, u32[]{:S(2)}) collective-permute-start(f32[2,64,128]{2,1,0:T(8,128)S(1)} %shard_map.78.refs_0_), channel_id=1, source_target_pairs={{0,16},{1,17},{2,18},{3,19},{4,20},{5,21},{6,22},{7,23},{8,24},{9,... | collective-permute-start | bytes 196616 | tf_op jit(solution)/shard_map/ppermute | solution.py:54
  62.1 6.7 %collective-permute-start.19 = (f32[2,64,128]{2,1,0:T(8,128)S(1)}, f32[2,64,128]{2,1,0:T(8,128)S(1)}, u32[]{:S(2)}, u32[]{:S(2)}) collective-permute-start(f32[2,64,128]{2,1,0:T(8,128)S(1)} %shard_map.78.refs_0_), channel_id=1, source_target_pairs={{0,24},{1,25},{2,26},{3,27},{4,28},{5,29},{6,30},{7,31},{8,16},{9,... | collective-permute-start | bytes 196616 | tf_op jit(solution)/shard_map/ppermute | solution.py:54
  69.2 35.8 %collective-permute-start.32 = (f32[256,4096]{1,0:T(8,128)S(1)}, f32[256,4096]{1,0:T(8,128)S(1)}, u32[]{:S(2)}, u32[]{:S(2)}) collective-permute-start(f32[256,4096]{1,0:T(8,128)S(1)} %shard_map.88), channel_id=1, source_target_pairs={{0,1},{1,0},{2,3},{3,2},{4,5},{5,4},{6,7},{7,6},{8,9},{9,8},{10,11... | collective-permute-start | bytes 12582920 | tf_op jit(solution)/shard_map/ppermute | solution.py:54
  69.5 36.6 %collective-permute-start.28 = (f32[4096,256]{1,0:T(8,128)S(1)}, f32[4096,256]{1,0:T(8,128)S(1)}, u32[]{:S(2)}, u32[]{:S(2)}) collective-permute-start(f32[4096,256]{1,0:T(8,128)S(1)} %shard_map.85), channel_id=1, source_target_pairs={{0,1},{1,0},{2,3},{3,2},{4,5},{5,4},{6,7},{7,6},{8,9},{9,8},{10,11... | collective-permute-start | bytes 12582920 | tf_op jit(solution)/shard_map/ppermute | solution.py:54
  70.1 5.5 %collective-permute-start.25 = (f32[4,64,128]{2,1,0:T(8,128)S(1)}, f32[4,64,128]{2,1,0:T(8,128)S(1)}, u32[]{:S(2)}, u32[]{:S(2)}) collective-permute-start(f32[4,64,128]{2,1,0:T(8,128)S(1)} %get-tuple-element.82.refs_0_), channel_id=1, source_target_pairs={{0,2},{1,3},{2,0},{3,1},{4,6},{5,7},{6,4},{7,5},{8,10},{9,11},{10,... | collective-permute-start | bytes 393224 | tf_op jit(solution)/shard_map/ppermute | solution.py:54
  71.1 5.6 %collective-permute-start.23 = (f32[4,64,128]{2,1,0:T(8,128)S(1)}, f32[4,64,128]{2,1,0:T(8,128)S(1)}, u32[]{:S(2)}, u32[]{:S(2)}) collective-permute-start(f32[4,64,128]{2,1,0:T(8,128)S(1)} %get-tuple-element.81.refs_0_.refs_1_), channel_id=1, source_target_pairs={{0,4},{1,5},{2,6},{3,7},{4,0},{5,1},{6,2},{7,3},{8,12},{9,13},{10,... | collective-permute-start | bytes 393224 | tf_op jit(solution)/shard_map/ppermute | solution.py:54
  75.6 7.5 %collective-permute-start.26 = (f32[8,64,128]{2,1,0:T(8,128)S(1)}, f32[8,64,128]{2,1,0:T(8,128)S(1)}, u32[]{:S(2)}, u32[]{:S(2)}) collective-permute-start(f32[8,64,128]{2,1,0:T(8,128)S(1)} %shard_map.82.refs_3_), channel_id=1, source_target_pairs={{0,4},{1,5},{2,6},{3,7},{4,0},{5,1},{6,2},{7,3},{8,12},{9,13},{10,... | collective-permute-start | bytes 786440 | tf_op jit(solution)/shard_map/ppermute | solution.py:54
  76.8 9.3 %collective-permute-start.24 = (f32[8,64,128]{2,1,0:T(8,128)S(1)}, f32[8,64,128]{2,1,0:T(8,128)S(1)}, u32[]{:S(2)}, u32[]{:S(2)}) collective-permute-start(f32[8,64,128]{2,1,0:T(8,128)S(1)} %shard_map.81.refs_1_), channel_id=1, source_target_pairs={{0,2},{1,3},{2,0},{3,1},{4,6},{5,7},{6,4},{7,5},{8,10},{9,11},{10,... | collective-permute-start | bytes 786440 | tf_op jit(solution)/shard_map/ppermute | solution.py:54
  78.6 12.0 %collective-permute-start.29 = (f32[4,2,64,128]{3,2,0,1:T(8,128)S(1)}, f32[4,2,64,128]{3,2,0,1:T(8,128)S(1)}, u32[]{:S(2)}, u32[]{:S(2)}) collective-permute-start(f32[4,2,64,128]{3,2,0,1:T(8,128)S(1)} %copy.7), channel_id=1, source_target_pairs={{0,4},{1,3},{2,6},{3,1},{4,0},{5,7},{6,2},{7,5},{8,12},{9,11},{10,... | collective-permute-start | bytes 786440 | tf_op jit(solution)/shard_map/ppermute | solution.py:54
  87.3 5.0 %collective-permute-start.33 = (f32[2,64,128]{2,1,0:T(8,128)S(1)}, f32[2,64,128]{2,1,0:T(8,128)S(1)}, u32[]{:S(2)}, u32[]{:S(2)}) collective-permute-start(f32[2,64,128]{2,1,0:T(8,128)S(1)} %get-tuple-element.83.refs_0_), channel_id=1, source_target_pairs={{0,8},{1,9},{2,10},{3,11},{4,12},{5,13},{6,14},{7,15},{8,0},{9,1},... | collective-permute-start | bytes 196616 | tf_op jit(solution)/shard_map/ppermute | solution.py:54
  88.2 5.9 %collective-permute-start.34 = (f32[2,64,128]{2,1,0:T(8,128)S(1)}, f32[2,64,128]{2,1,0:T(8,128)S(1)}, u32[]{:S(2)}, u32[]{:S(2)}) collective-permute-start(f32[2,64,128]{2,1,0:T(8,128)S(1)} %get-tuple-element.83.refs_0_), channel_id=1, source_target_pairs={{0,16},{1,17},{2,18},{3,19},{4,20},{5,21},{6,22},{7,23},{8,24},{9,... | collective-permute-start | bytes 196616 | tf_op jit(solution)/shard_map/ppermute | solution.py:54
  90.6 6.2 %collective-permute-start.35 = (f32[2,64,128]{2,1,0:T(8,128)S(1)}, f32[2,64,128]{2,1,0:T(8,128)S(1)}, u32[]{:S(2)}, u32[]{:S(2)}) collective-permute-start(f32[2,64,128]{2,1,0:T(8,128)S(1)} %get-tuple-element.83.refs_0_), channel_id=1, source_target_pairs={{0,24},{1,25},{2,26},{3,27},{4,28},{5,29},{6,30},{7,31},{8,16},{9,... | collective-permute-start | bytes 196616 | tf_op jit(solution)/shard_map/ppermute | solution.py:54
  96.7 5.0 %collective-permute-start.38 = (f32[4,64,128]{2,1,0:T(8,128)S(1)}, f32[4,64,128]{2,1,0:T(8,128)S(1)}, u32[]{:S(2)}, u32[]{:S(2)}) collective-permute-start(f32[4,64,128]{2,1,0:T(8,128)S(1)} %get-tuple-element.91.refs_0_), channel_id=1, source_target_pairs={{0,2},{1,3},{2,0},{3,1},{4,6},{5,7},{6,4},{7,5},{8,10},{9,11},{10,... | collective-permute-start | bytes 393224 | tf_op jit(solution)/shard_map/ppermute | solution.py:54
  97.3 5.0 %collective-permute-start.36 = (f32[4,64,128]{2,1,0:T(8,128)S(1)}, f32[4,64,128]{2,1,0:T(8,128)S(1)}, u32[]{:S(2)}, u32[]{:S(2)}) collective-permute-start(f32[4,64,128]{2,1,0:T(8,128)S(1)} %get-tuple-element.90.refs_0_), channel_id=1, source_target_pairs={{0,4},{1,5},{2,6},{3,7},{4,0},{5,1},{6,2},{7,3},{8,12},{9,13},{10,... | collective-permute-start | bytes 393224 | tf_op jit(solution)/shard_map/ppermute | solution.py:54
  98.4 5.0 %collective-permute-start.30 = (f32[2,2,64,128]{3,2,0,1:T(8,128)S(1)}, f32[2,2,64,128]{3,2,0,1:T(8,128)S(1)}, u32[]{:S(2)}, u32[]{:S(2)}) collective-permute-start(f32[2,2,64,128]{3,2,0,1:T(8,128)S(1)} %slice.31), channel_id=1, source_target_pairs={{0,8},{1,9},{2,10},{3,11},{4,12},{5,13},{6,14},{7,15},{8,0},{9,1},... | collective-permute-start | bytes 393224 | tf_op jit(solution)/shard_map/ppermute | solution.py:54
  101.8 2.4 %collective-permute-start.27 = (f32[1,64,128]{2,1,0:T(8,128)S(1)}, f32[1,64,128]{2,1,0:T(8,128)S(1)}, u32[]{:S(2)}, u32[]{:S(2)}) collective-permute-start(f32[1,64,128]{2,1,0:T(8,128)S(1)} %get-tuple-element.84), channel_id=1, source_target_pairs={{0,1},{1,0},{2,3},{3,2},{4,5},{5,4},{6,7},{7,6},{8,9},{9,8},{10,11... | collective-permute-start | bytes 98312 | tf_op jit(solution)/shard_map/ppermute | solution.py:54
  102.2 8.4 %collective-permute-start.39 = (f32[8,64,128]{2,1,0:T(8,128)S(1)}, f32[8,64,128]{2,1,0:T(8,128)S(1)}, u32[]{:S(2)}, u32[]{:S(2)}) collective-permute-start(f32[8,64,128]{2,1,0:T(8,128)S(1)} %shard_map.92.refs_3_), channel_id=1, source_target_pairs={{0,4},{1,5},{2,6},{3,7},{4,0},{5,1},{6,2},{7,3},{8,12},{9,13},{10,... | collective-permute-start | bytes 786440 | tf_op jit(solution)/shard_map/ppermute | solution.py:54
  103.5 7.2 %collective-permute-start.37 = (f32[8,64,128]{2,1,0:T(8,128)S(1)}, f32[8,64,128]{2,1,0:T(8,128)S(1)}, u32[]{:S(2)}, u32[]{:S(2)}) collective-permute-start(f32[8,64,128]{2,1,0:T(8,128)S(1)} %shard_map.91.refs_1_), channel_id=1, source_target_pairs={{0,2},{1,3},{2,0},{3,1},{4,6},{5,7},{6,4},{7,5},{8,10},{9,11},{10,... | collective-permute-start | bytes 786440 | tf_op jit(solution)/shard_map/ppermute | solution.py:54
  104.2 8.3 %collective-permute-start.31 = (f32[2,64,128]{2,1,0:T(8,128)S(1)}, f32[2,64,128]{2,1,0:T(8,128)S(1)}, u32[]{:S(2)}, u32[]{:S(2)}) collective-permute-start(f32[2,64,128]{2,1,0:T(8,128)S(1)} %get-tuple-element.104), channel_id=1, source_target_pairs={{0,1},{1,0},{2,3},{3,2},{4,5},{5,4},{6,7},{7,6},{8,9},{9,8},{10,11... | collective-permute-start | bytes 196616 | tf_op jit(solution)/shard_map/ppermute | solution.py:54
  114.0 7.5 %collective-permute-start.42 = (f32[8,64,128]{2,1,0:T(8,128)S(1)}, f32[8,64,128]{2,1,0:T(8,128)S(1)}, u32[]{:S(2)}, u32[]{:S(2)}) collective-permute-start(f32[8,64,128]{2,1,0:T(8,128)S(1)} %get-tuple-element.96), channel_id=1, source_target_pairs={{0,4},{1,5},{2,6},{3,7},{4,0},{5,1},{6,2},{7,3},{8,12},{9,13},{10,... | collective-permute-start | bytes 786440 | tf_op jit(solution)/shard_map/ppermute | solution.py:54
  115.8 7.1 %collective-permute-start.40 = (f32[8,64,128]{2,1,0:T(8,128)S(1)}, f32[8,64,128]{2,1,0:T(8,128)S(1)}, u32[]{:S(2)}, u32[]{:S(2)}) collective-permute-start(f32[8,64,128]{2,1,0:T(8,128)S(1)} %get-tuple-element.93), channel_id=1, source_target_pairs={{0,2},{1,3},{2,0},{3,1},{4,6},{5,7},{6,4},{7,5},{8,10},{9,11},{10,... | collective-permute-start | bytes 786440 | tf_op jit(solution)/shard_map/ppermute | solution.py:54
  121.5 5.0 %collective-permute-start.43 = (f32[4,64,128]{2,1,0:T(8,128)S(1)}, f32[4,64,128]{2,1,0:T(8,128)S(1)}, u32[]{:S(2)}, u32[]{:S(2)}) collective-permute-start(f32[4,64,128]{2,1,0:T(8,128)S(1)} %shard_map.96), channel_id=1, source_target_pairs={{0,2},{1,3},{2,0},{3,1},{4,6},{5,7},{6,4},{7,5},{8,10},{9,11},{10,... | collective-permute-start | bytes 393224 | tf_op jit(solution)/shard_map/ppermute | solution.py:54
  122.9 5.0 %collective-permute-start.41 = (f32[4,64,128]{2,1,0:T(8,128)S(1)}, f32[4,64,128]{2,1,0:T(8,128)S(1)}, u32[]{:S(2)}, u32[]{:S(2)}) collective-permute-start(f32[4,64,128]{2,1,0:T(8,128)S(1)} %shard_map.95), channel_id=1, source_target_pairs={{0,4},{1,5},{2,6},{3,7},{4,0},{5,1},{6,2},{7,3},{8,12},{9,13},{10,... | collective-permute-start | bytes 393224 | tf_op jit(solution)/shard_map/ppermute | solution.py:54
  128.0 6.4 %collective-permute-start.44 = (f32[4,2,64,128]{3,2,1,0:T(8,128)S(1)}, f32[4,2,64,128]{3,2,1,0:T(8,128)S(1)}, u32[]{:S(2)}, u32[]{:S(2)}) collective-permute-start(f32[4,2,64,128]{3,2,1,0:T(8,128)S(1)} %get-tuple-element.99), channel_id=1, source_target_pairs={{0,8},{1,9},{2,10},{3,11},{4,12},{5,13},{6,14},{7,15},{8,0},{9,1},... | collective-permute-start | bytes 786440 | tf_op jit(solution)/shard_map/ppermute | solution.py:54
  134.5 6.4 %collective-permute-start.47 = (f32[4,64,128]{2,1,0:T(8,128)S(1)}, f32[4,64,128]{2,1,0:T(8,128)S(1)}, u32[]{:S(2)}, u32[]{:S(2)}) collective-permute-start(f32[4,64,128]{2,1,0:T(8,128)S(1)} %get-tuple-element.101.refs_0_), channel_id=1, source_target_pairs={{0,2},{1,3},{2,0},{3,1},{4,6},{5,7},{6,4},{7,5},{8,10},{9,11},{10,... | collective-permute-start | bytes 393224 | tf_op jit(solution)/shard_map/ppermute | solution.py:54
  135.2 5.8 %collective-permute-start.45 = (f32[4,64,128]{2,1,0:T(8,128)S(1)}, f32[4,64,128]{2,1,0:T(8,128)S(1)}, u32[]{:S(2)}, u32[]{:S(2)}) collective-permute-start(f32[4,64,128]{2,1,0:T(8,128)S(1)} %get-tuple-element.100.refs_0_), channel_id=1, source_target_pairs={{0,4},{1,5},{2,6},{3,7},{4,0},{5,1},{6,2},{7,3},{8,12},{9,13},{10,... | collective-permute-start | bytes 393224 | tf_op jit(solution)/shard_map/ppermute | solution.py:54
  140.9 6.4 %collective-permute-start.48 = (f32[8,64,128]{2,1,0:T(8,128)S(1)}, f32[8,64,128]{2,1,0:T(8,128)S(1)}, u32[]{:S(2)}, u32[]{:S(2)}) collective-permute-start(f32[8,64,128]{2,1,0:T(8,128)S(1)} %shard_map.100.refs_3_), channel_id=1, source_target_pairs={{0,4},{1,5},{2,6},{3,7},{4,0},{5,1},{6,2},{7,3},{8,12},{9,13},{10,... | collective-permute-start | bytes 786440 | tf_op jit(solution)/shard_map/ppermute | solution.py:54
  141.0 6.6 %collective-permute-start.46 = (f32[8,64,128]{2,1,0:T(8,128)S(1)}, f32[8,64,128]{2,1,0:T(8,128)S(1)}, u32[]{:S(2)}, u32[]{:S(2)}) collective-permute-start(f32[8,64,128]{2,1,0:T(8,128)S(1)} %shard_map.99.refs_1_), channel_id=1, source_target_pairs={{0,2},{1,3},{2,0},{3,1},{4,6},{5,7},{6,4},{7,5},{8,10},{9,11},{10,... | collective-permute-start | bytes 786440 | tf_op jit(solution)/shard_map/ppermute | solution.py:54
  (10 other events, 103.9 us)
